TPU v7x, 256 devices: a whole 4x4x8 slice. The times are simulated.
256 devices in a mesh: expert: 16 (over z_hi, y, core), space: 16 (over x, z_lo).
Axes of the slice: x: 4, y: 4, z: 8 (z_hi: 2, z_lo: 4; z = z_hi * 4 + z_lo), core: 2. Of those that a mesh axis runs over, the one named last changes fastest.
Arguments:
- attn_inputs: bfloat16 [3, 16, 192, 12, 512], P(None, 'expert', 'space'), may hold values from -9 to 9
- residual: bfloat16 [16, 192, 12, 512], P('expert', 'space'), may hold values from -400 to 400
- logits: float32 [16, 192, 12, 32], P('expert', 'space'), may hold values from -12 to 454
- expert_ids: int32 [16, 192, 12, 2], P('expert', 'space'), may hold values from 0 to 31, all different within a row; in each aligned block of 144 rows (0 to 143, 144 to 287, ..., all dimensions but the last counted through in order) at most 12 rows name the same one
- keep_mask: int32 [16, 192, 12, 2], P('expert', 'space'), may hold values 0 or 1
- cotangent: bfloat16 [16, 192, 12, 512], P('expert', 'space'), may hold values from -1.5 to 1.5
- up_weight: bfloat16 [32, 512, 2048], P('expert', None, 'space'), may hold values from -0.25 to 0.25
- down_weight: bfloat16 [32, 512, 2048], P('expert', None, 'space'), may hold values from -0.125 to 0.125
Outputs:
- attn_grad: bfloat16 [3, 16, 192, 12, 512], P(None, 'expert', 'space')
- residual_grad: bfloat16 [16, 192, 12, 512], P('expert', 'space')
- up_grad: float32 [32, 512, 2048], P('expert', None, 'space')
- down_grad: float32 [32, 512, 2048], P('expert', None, 'space')
- logit_grad: float32 [16, 192, 12, 32], P('expert', 'space')
Inputs may be any that keep to these rules, and one draw needn't show every extreme that they name: `expert_ids`: each token names 2 different experts; among the tokens of one strip no expert is named more than 12 times, and in every draw some expert is named exactly 12 times by the tokens of some strip.
All inputs are finite; a program needn't handle non-finite values. No bound on the sum of `keep_mask` on one device may be relied on, other than what follows from the above.
Results may differ from a plain program's by a relative error of at most 0.012.
Values may be sent and summed in bfloat16 or wider, within the bound.
A program may use at most 128 MiB of HBM per device.

v0:
```python
import jax
import jax.numpy as jnp
from jax import lax
from jax.sharding import PartitionSpec as P

HEADS = 16
EXPERTS = 32
TOP = 2
CAP = 12


NORM_EPS = 1e-06
SCORE_MASK = -100.0


def from_behind(block, axis, distance):
    devices = range(lax.axis_size(axis))
    route = [((i - distance) % len(devices), i) for i in devices]
    return lax.ppermute(block, axis, route)


def gelu_pair(pre_act):
    activation, pullback = jax.vjp(jax.nn.gelu, pre_act)
    gelu_slope = pullback(jnp.ones_like(pre_act))[0]
    return (activation, gelu_slope)


def to_windows(tensor, head_count):
    blocks, win_side, map_width, channels = tensor.shape
    win_count = map_width // win_side
    head_dim = channels // head_count
    shaped = tensor.reshape(blocks, win_side, win_count, win_side, head_count, head_dim)
    shaped = shaped.transpose(0, 2, 4, 1, 3, 5)
    return shaped.reshape(blocks, win_count, head_count, win_side * win_side, head_dim)


def from_windows(tensor, win_side):
    blocks, win_count, head_count, win_area, head_dim = tensor.shape
    shaped = tensor.reshape(blocks, win_count, head_count, win_side, win_side, head_dim)
    shaped = shaped.transpose(0, 3, 1, 4, 2, 5)
    return shaped.reshape(blocks, win_side, win_count * win_side, head_count * head_dim)


def window_grads(frame_qkv, frame_grad, last_flags, head_count):
    win_side = frame_grad.shape[1]
    map_width = frame_grad.shape[2]
    half_win = win_side // 2
    head_dim = frame_grad.shape[3] // head_count
    inv_sqrt = head_dim ** (-0.5)
    rolled = jnp.roll(frame_qkv, -half_win, axis=3)
    grad_rolled = jnp.roll(frame_grad, -half_win, axis=2)
    query_win = to_windows(rolled[0], head_count)
    key_win = to_windows(rolled[1], head_count)
    value_win = to_windows(rolled[2], head_count)
    grad_win = to_windows(grad_rolled, head_count)
    row_pos = jnp.arange(win_side, dtype=jnp.int32)
    col_pos = jnp.arange(map_width, dtype=jnp.int32)
    row_label = jnp.where(last_flags[:, None], jnp.where(row_pos < half_win, 1, 2)[None, :], 0)
    col_label = jnp.where(
        col_pos >= map_width - win_side, jnp.where(col_pos < map_width - half_win, 1, 2), 0
    )
    region = 3 * row_label[:, :, None] + col_label[None, None, :]
    region = region.reshape(region.shape[0], win_side, map_width // win_side, win_side).transpose(
        0, 2, 1, 3
    )
    region = region.reshape(region.shape[0], region.shape[1], win_side * win_side)
    score_bias = jnp.where(region[:, :, :, None] != region[:, :, None, :], SCORE_MASK, 0.0)[
        :, :, None
    ]
    scores = (
        jnp.einsum("bnhqd,bnhkd->bnhqk", query_win, key_win, preferred_element_type=jnp.float32)
        * inv_sqrt
        + score_bias
    )
    row_max = jnp.max(scores, axis=-1, keepdims=True)
    exp_scores = jnp.exp(scores - row_max)
    attn_probs = exp_scores / jnp.sum(exp_scores, axis=-1, keepdims=True)
    weights_bf = attn_probs.astype(jnp.bfloat16)
    attn_out = jnp.einsum(
        "bnhqk,bnhkd->bnhqd", weights_bf, value_win, preferred_element_type=jnp.float32
    )
    row_delta = jnp.sum(grad_win.astype(jnp.float32) * attn_out, axis=-1, keepdims=True)
    prob_grad = jnp.einsum(
        "bnhqd,bnhkd->bnhqk", grad_win, value_win, preferred_element_type=jnp.float32
    )
    score_grad = (attn_probs * (prob_grad - row_delta)).astype(jnp.bfloat16)
    query_grad = (
        jnp.einsum("bnhqk,bnhkd->bnhqd", score_grad, key_win, preferred_element_type=jnp.float32)
        * inv_sqrt
    ).astype(jnp.bfloat16)
    key_grad = (
        jnp.einsum("bnhqk,bnhqd->bnhkd", score_grad, query_win, preferred_element_type=jnp.float32)
        * inv_sqrt
    ).astype(jnp.bfloat16)
    value_grad = jnp.einsum(
        "bnhqk,bnhqd->bnhkd", weights_bf, grad_win, preferred_element_type=jnp.float32
    ).astype(jnp.bfloat16)
    stacked = jnp.stack(
        [
            from_windows(query_grad, win_side),
            from_windows(key_grad, win_side),
            from_windows(value_grad, win_side),
        ]
    )
    return jnp.roll(stacked, half_win, axis=3)


def per_device(
    attn_inputs, residual, logits, expert_ids, keep_mask, cotangent, up_weight, down_weight
):
    group_count = lax.axis_size("expert")
    local_experts = up_weight.shape[0]
    win_side = residual.shape[1]
    map_width = residual.shape[2]
    channels = residual.shape[3]
    tokens = win_side * map_width
    half_win = win_side // 2
    space_index = lax.axis_index("space")
    space_count = lax.axis_size("space")
    qkv_local = attn_inputs[:, 0]
    next_rows = from_behind(qkv_local[:, :half_win], "space", -1)
    qkv_shifted = jnp.concatenate([qkv_local[:, half_win:], next_rows], axis=1)
    resid_float = residual[0].reshape(tokens, channels).astype(jnp.float32)
    rms_value = jnp.sqrt(jnp.mean(resid_float * resid_float, axis=-1, keepdims=True) + NORM_EPS)
    norm_float = resid_float / rms_value
    normed = norm_float.astype(jnp.bfloat16)
    route_ids = expert_ids[0].reshape(tokens, TOP)
    keep_float = keep_mask[0].reshape(tokens, TOP).astype(jnp.float32)
    router_logits = logits[0].reshape(tokens, EXPERTS)
    expert_cols = jnp.arange(EXPERTS, dtype=jnp.int32)
    one_hot = route_ids[:, :, None] == expert_cols[None, None, :]
    chosen = jnp.sum(jnp.where(one_hot, router_logits[:, None, :], 0.0), axis=-1)
    chosen_max = jnp.max(chosen, axis=-1, keepdims=True)
    chosen_exp = jnp.exp(chosen - chosen_max)
    gates_top = chosen_exp / jnp.sum(chosen_exp, axis=-1, keepdims=True)
    gate_weight = gates_top * keep_float
    cot_rows = cotangent[0].reshape(tokens, channels)
    scaled_rows = (gate_weight[:, :, None] * cot_rows[:, None, :].astype(jnp.float32)).astype(
        jnp.bfloat16
    )
    flat_hot = one_hot.reshape(tokens * TOP, EXPERTS).astype(jnp.int32)
    running = jnp.cumsum(flat_hot, axis=0) - flat_hot
    slot_index = jnp.sum(running * flat_hot, axis=-1)
    flat_ids = route_ids.reshape(-1)
    destination = (
        flat_ids % local_experts * group_count + flat_ids // local_experts
    ) * CAP + slot_index
    slot_total = local_experts * group_count * CAP
    choice_norm = jnp.broadcast_to(normed[:, None, :], (tokens, TOP, channels)).reshape(
        tokens * TOP, channels
    )
    choice_cot = jnp.broadcast_to(cot_rows[:, None, :], (tokens, TOP, channels)).reshape(
        tokens * TOP, channels
    )
    send_norm = (
        jnp.zeros((slot_total, channels), jnp.bfloat16)
        .at[destination]
        .set(choice_norm)
        .reshape(local_experts, group_count, CAP, channels)
    )
    send_cot = (
        jnp.zeros((slot_total, channels), jnp.bfloat16)
        .at[destination]
        .set(choice_cot)
        .reshape(local_experts, group_count, CAP, channels)
    )
    send_scaled = (
        jnp.zeros((slot_total, channels), jnp.bfloat16)
        .at[destination]
        .set(scaled_rows.reshape(tokens * TOP, channels))
        .reshape(local_experts, group_count, CAP, channels)
    )
    recv_norm, recv_cot, recv_scaled = (
        lax.all_to_all(send_norm, "expert", split_axis=1, concat_axis=1, tiled=True),
        lax.all_to_all(send_cot, "expert", split_axis=1, concat_axis=1, tiled=True),
        lax.all_to_all(send_scaled, "expert", split_axis=1, concat_axis=1, tiled=True),
    )
    expert_rows = group_count * CAP
    in_rows = recv_norm.reshape(local_experts, expert_rows, channels)
    cot_in = recv_cot.reshape(local_experts, expert_rows, channels)
    scaled = recv_scaled.reshape(local_experts, expert_rows, channels)
    up_piece = lax.all_gather(up_weight, "space", axis=2, tiled=True)
    down_piece = lax.all_gather(down_weight, "space", axis=2, tiled=True)
    pre_act = jnp.einsum("erc,ecf->erf", in_rows, up_piece, preferred_element_type=jnp.float32)
    activation, gelu_slope = gelu_pair(pre_act)
    act_bf = activation.astype(jnp.bfloat16)
    out_sum = jnp.einsum("erf,ecf->erc", act_bf, down_piece, preferred_element_type=jnp.float32)
    pre_grad = (
        jnp.einsum("erc,ecf->erf", scaled, down_piece, preferred_element_type=jnp.float32)
        * gelu_slope
    ).astype(jnp.bfloat16)
    grad_sum = jnp.einsum("erf,ecf->erc", pre_grad, up_piece, preferred_element_type=jnp.float32)
    up_term = jnp.einsum("erc,erf->ecf", in_rows, pre_grad, preferred_element_type=jnp.float32)
    down_term = jnp.einsum("erc,erf->ecf", scaled, act_bf, preferred_element_type=jnp.float32)
    first_store = up_term
    second_store = down_term
    out_sum, grad_sum, first_store, second_store = (out_sum, grad_sum, first_store, second_store)
    row_dots = jnp.sum(cot_in.astype(jnp.float32) * out_sum, axis=-1).astype(jnp.bfloat16)
    back_grad = grad_sum.astype(jnp.bfloat16).reshape(local_experts, group_count, CAP, channels)
    ret_grad, ret_dots = (
        lax.all_to_all(back_grad, "expert", split_axis=1, concat_axis=1, tiled=True),
        lax.all_to_all(
            row_dots.reshape(local_experts, group_count, CAP),
            "expert",
            split_axis=1,
            concat_axis=1,
            tiled=True,
        ),
    )
    up_grad, down_grad = (
        lax.psum_scatter(first_store, "space", scatter_dimension=2, tiled=True),
        lax.psum_scatter(second_store, "space", scatter_dimension=2, tiled=True),
    )
    choice_grad = (
        ret_grad.reshape(slot_total, channels)[destination]
        .astype(jnp.float32)
        .reshape(tokens, TOP, channels)
    )
    norm_grad = jnp.sum(choice_grad, axis=1)
    inner_mean = jnp.mean(norm_grad * norm_float, axis=-1, keepdims=True)
    residual_grad = (
        cot_rows.astype(jnp.float32) + (norm_grad - norm_float * inner_mean) / rms_value
    ).astype(jnp.bfloat16)
    choice_dots = ret_dots.reshape(slot_total)[destination].astype(jnp.float32).reshape(tokens, TOP)
    gate_drive = keep_float * choice_dots
    gate_mix = jnp.sum(gates_top * gate_drive, axis=-1, keepdims=True)
    gate_part = gates_top * (gate_drive - gate_mix)
    logit_gate = jnp.sum(jnp.where(one_hot, gate_part[:, :, None], 0.0), axis=1)
    expert_share = jnp.sum(jnp.where(one_hot, keep_float[:, :, None], 0.0), axis=(0, 1)) / (
        TOP * tokens
    )
    logit_max = jnp.max(router_logits, axis=-1, keepdims=True)
    logit_exp = jnp.exp(router_logits - logit_max)
    router_probs = logit_exp / jnp.sum(logit_exp, axis=-1, keepdims=True)
    share_mean = jnp.sum(router_probs * expert_share[None, :], axis=-1, keepdims=True)
    balance = EXPERTS * router_probs * (expert_share[None, :] - share_mean)
    logit_grad = (logit_gate + balance).reshape(1, win_side, map_width, EXPERTS)
    grad_map = residual_grad.reshape(win_side, map_width, channels)
    next_grad = from_behind(grad_map[:half_win], "space", -1)
    grad_shifted = jnp.concatenate([grad_map[half_win:], next_grad], axis=0)
    last_flags = jnp.reshape(space_index == space_count - 1, (1,))
    frame_grads = window_grads(qkv_shifted[:, None], grad_shifted[None], last_flags, HEADS)[:, 0]
    prev_rows = from_behind(frame_grads[:, half_win:], "space", 1)
    attn_grad = jnp.concatenate([prev_rows, frame_grads[:, :half_win]], axis=1)
    return (attn_grad[:, None], grad_map[None], up_grad, down_grad, logit_grad)


def solution(mesh):
    in_specs = (
        P(None, "expert", "space", None, None),
        P("expert", "space", None, None),
        P("expert", "space", None, None),
        P("expert", "space", None, None),
        P("expert", "space", None, None),
        P("expert", "space", None, None),
        P("expert", None, "space"),
        P("expert", None, "space"),
    )
    out_specs = (
        P(None, "expert", "space", None, None),
        P("expert", "space", None, None),
        P("expert", None, "space"),
        P("expert", None, "space"),
        P("expert", "space", None, None),
    )
    return jax.shard_map(
        per_device, mesh=mesh, in_specs=in_specs, out_specs=out_specs, check_vma=False
    )
```

profile of v0, /device:TPU:24, one launch (start us, length us, event | category | flops | bytes accessed | tf_op | source)
XLA Modules:
  0.0 736.4 jit_solution(12673675491720446703)
XLA Ops:
  12.4 1.7 scatter_custom_fusion.2
  15.4 11.5 %all-to-all-start.3 = ((bf16[2,16,12,512]{3,0,2,1:T(2,128)(2,1)}), bf16[2,16,12,512]{3,0,2,1:T(2,128)(2,1)S(1)}, u32[]{:S(2)}, u32[]{:S(2)}) async-start(bf16[2,16,12,512]{3,0,2,1:T(2,128)(2,1)} %copy.195), calls=%async_computation.5 | async-start | bytes 786432 | tf_op jit(solution)/shard_map/all_to_all | solution.py:175
  27.5 1.7 scatter_custom_fusion.1
  30.5 13.7 %all-to-all-done.3 = bf16[2,16,12,512]{3,0,2,1:T(2,128)(2,1)S(1)} async-done(((bf16[2,16,12,512]{3,0,2,1:T(2,128)(2,1)}), bf16[2,16,12,512]{3,0,2,1:T(2,128)(2,1)S(1)}, u32[]{:S(2)}, u32[]{:S(2)}) %all-to-all-start.3) | async-done | bytes 393248 | tf_op jit(solution)/shard_map/all_to_all | solution.py:175
  44.3 5.8 all-to-all-start.1
  52.1 10.5 %all-to-all-done.1 = bf16[2,16,12,512]{3,0,2,1:T(2,128)(2,1)S(1)} async-done(((bf16[2,16,12,512]{3,0,2,1:T(2,128)(2,1)}), bf16[2,16,12,512]{3,0,2,1:T(2,128)(2,1)S(1)}, u32[]{:S(2)}, u32[]{:S(2)}) %all-to-all-start.1) | async-done | bytes 393248 | tf_op jit(solution)/shard_map/all_to_all | solution.py:174
  62.7 75.9 %all-gather.5.cloned.1.call-done = bf16[2,512,2048]{2,1,0:T(8,128)(2,1)} async-done(((bf16[2,512,128]{2,1,0:T(8,128)(2,1)}), bf16[2,512,2048]{2,1,0:T(8,128)(2,1)}) %all-gather.5.cloned.1.call-update) | async-done | bytes 4194320 | tf_op jit(solution)/shard_map/all_gather | solution.py:182
  138.6 3.2 fusion.19
  141.8 112.6 %all-gather.3.cloned.1.call-done = bf16[2,512,2048]{2,1,0:T(8,128)(2,1)} async-done(((bf16[2,512,128]{2,1,0:T(8,128)(2,1)}), bf16[2,512,2048]{2,1,0:T(8,128)(2,1)}) %all-gather.3.cloned.1.call-update) | async-done | bytes 4194320 | tf_op jit(solution)/shard_map/all_gather | solution.py:183
  254.4 4.7 fusion.10
  259.1 1.4 convert_element_type.171
  260.5 1.3 copy.197
  261.8 5.4 all-to-all-start.4
  267.4 1.3 pad_clamp_fusion
  268.7 1.3 sub.121
  270.0 1.4 reduce_sum.145
  272.8 1.4 div.118
  274.2 1.6 convert_element_type.147
  275.8 1.9 mul.197
  277.7 2.3 mul.198
  280.8 2.6 gather_fusion.1
  286.0 1.4 multiply_reduce_fusion.3
  292.3 2.9 scatter_custom_fusion
  295.2 1.9 reshape.671
  297.1 1.4 copy.169
  298.5 20.8 %all_to_all.25 = bf16[2,16,12,512]{3,0,2,1:T(2,128)(2,1)S(1)} all-to-all(bf16[2,16,12,512]{3,0,2,1:T(2,128)(2,1)S(1)} %copy.169), channel_id=1, replica_groups=mesh['expert'=16,'space'=16] {'expert'}, dimensions={1} | all-to-all | bytes 786432 | tf_op jit(solution)/shard_map/all_to_all | solution.py:176
  319.4 5.6 fusion.8
  326.2 4.5 fusion.17
  331.7 4.6 fusion.21
  337.4 5.7 collective-permute-start
  344.7 12.7 %collective-permute-done = bf16[3,6,12,512]{3,2,1,0:T(8,128)(2,1)S(1)} collective-permute-done((bf16[3,6,12,512]{3,2,1,0:T(8,128)(2,1)S(1)}, bf16[3,6,12,512]{3,2,1,0:T(8,128)(2,1)S(1)}, u32[]{:S(2)}, u32[]{:S(2)}) %collective-permute-start) | collective-permute-done | bytes 221216 | tf_op jit(solution)/shard_map/ppermute | solution.py:19
  359.8 1.2 copy.176
  361.0 3.3 fusion.55
  364.3 3.8 convolution_convert_fusion
  369.2 7.9 %all-to-all-start.2 = ((bf16[2,16,12,512]{3,0,2,1:T(2,128)(2,1)}), bf16[2,16,12,512]{3,0,2,1:T(2,128)(2,1)S(1)}, u32[]{:S(2)}, u32[]{:S(2)}) async-start(bf16[2,16,12,512]{3,0,2,1:T(2,128)(2,1)} %bitcast.10), calls=%async_computation.2 | async-start | bytes 786432 | tf_op jit(solution)/shard_map/all_to_all | solution.py:201
  377.1 1.9 fusion.16
  380.1 14.3 %all-to-all-done.2 = bf16[2,16,12,512]{3,0,2,1:T(2,128)(2,1)S(1)} async-done(((bf16[2,16,12,512]{3,0,2,1:T(2,128)(2,1)}), bf16[2,16,12,512]{3,0,2,1:T(2,128)(2,1)S(1)}, u32[]{:S(2)}, u32[]{:S(2)}) %all-to-all-start.2) | async-done | bytes 393248 | tf_op jit(solution)/shard_map/all_to_all | solution.py:201
  394.6 2.0 gather_fusion
  398.3 7.2 collective-permute-start.1
  407.3 11.1 %collective-permute-done.1 = bf16[6,12,512]{2,1,0:T(8,128)(2,1)S(1)} collective-permute-done((bf16[6,12,512]{2,1,0:T(8,128)(2,1)S(1)}, bf16[6,12,512]{2,1,0:T(8,128)(2,1)S(1)}, u32[]{:S(2)}, u32[]{:S(2)}) %collective-permute-start.1) | collective-permute-done | bytes 73760 | tf_op jit(solution)/shard_map/ppermute | solution.py:19
  419.7 2.3 multiply_convert_fusion.1
  423.1 1.4 copy.183
  424.5 1.2 stack_reshape.9
  425.8 1.5 fusion.11
  430.3 1.7 collective-permute-start.2
  432.8 16.9 %collective-permute-done.2 = bf16[3,6,12,512]{3,2,1,0:T(8,128)(2,1)S(1)} collective-permute-done((bf16[3,6,12,512]{3,2,1,0:T(8,128)(2,1)S(1)}, bf16[3,6,12,512]{3,2,1,0:T(8,128)(2,1)S(1)}, u32[]{:S(2)}, u32[]{:S(2)}) %collective-permute-start.2) | collective-permute-done | bytes 221216 | tf_op jit(solution)/shard_map/ppermute | solution.py:19
  450.6 90.1 %reduce-scatter.3.cloned.1.call-done = f32[2,512,128]{2,1,0:T(8,128)} async-done(((f32[2,512,2048]{2,1,0:T(8,128)}), f32[2,512,128]{2,1,0:T(8,128)}) %reduce-scatter.3.cloned.1.call-update) | async-done | bytes 524304 | tf_op jit(solution)/shard_map/reduce_scatter | solution.py:211
  540.8 189.1 %reduce-scatter.5.cloned.1.call-done = f32[2,512,128]{2,1,0:T(8,128)} async-done(((f32[2,512,2048]{2,1,0:T(8,128)}), f32[2,512,128]{2,1,0:T(8,128)}) %reduce-scatter.5.cloned.1.call-update) | async-done | bytes 524304 | tf_op jit(solution)/shard_map/reduce_scatter | solution.py:212
  (176 shorter events, 40.1 us)
Async XLA Ops:
  7.2 19.7 %copy-start.2 = (bf16[1,12,12,512]{3,2,1,0:T(8,128)(2,1)S(1)}, bf16[1,12,12,512]{3,2,1,0:T(8,128)(2,1)}, u32[]{:S(2)}) copy-start(bf16[1,12,12,512]{3,2,1,0:T(8,128)(2,1)} %param.9) | copy-start | bytes 442372
  7.2 131.4 %all-gather.5.cloned.1.call-start = ((), (), s32[]{:S(2)}) async-start(), calls=%async_computation.8 | async-start | bytes 4456448 | tf_op jit(solution)/shard_map/all_gather | solution.py:182
  7.9 246.5 %all-gather.3.cloned.1.call-start = ((), (), s32[]{:S(2)}) async-start(), calls=%async_computation.7 | async-start | bytes 4456448 | tf_op jit(solution)/shard_map/all_gather | solution.py:183
  12.0 15.6 %copy-start.6 = (bf16[144,512]{1,0:T(8,128)(2,1)}, bf16[144,512]{1,0:T(8,128)(2,1)S(1)}, u32[]{:S(2)}) copy-start(bf16[144,512]{1,0:T(8,128)(2,1)S(1)} %reshape_squeeze.17) | copy-start | bytes 442372
  12.4 17.0 %copy-start.31 = (s32[288]{0:T(512)}, s32[288]{0:T(512)S(1)}, u32[]{:S(2)}) copy-start(s32[288]{0:T(512)S(1)} %fusion.41) | copy-start | bytes 3460
  15.4 34.7 %copy-start.22 = (s32[1,12,12,2]{2,3,1,0:T(2,128)S(1)}, s32[1,12,12,2]{2,3,1,0:T(2,128)}, u32[]{:S(2)}) copy-start(s32[1,12,12,2]{2,3,1,0:T(2,128)} %param.11) | copy-start | bytes 3460
  15.4 34.8 %copy-start.10 = (f32[1,12,12,32]{3,0,2,1:T(1,128)S(1)}, f32[1,12,12,32]{3,0,2,1:T(1,128)}, u32[]{:S(2)}) copy-start(f32[1,12,12,32]{3,0,2,1:T(1,128)} %param.10) | copy-start | bytes 55300
  15.4 35.6 %copy-start.23 = (s32[1,12,12,2]{2,3,1,0:T(2,128)S(1)}, s32[1,12,12,2]{2,3,1,0:T(2,128)}, u32[]{:S(2)}) copy-start(s32[1,12,12,2]{2,3,1,0:T(2,128)} %param.12) | copy-start | bytes 3460
  15.4 28.9 %all-to-all-start.3 = ((bf16[2,16,12,512]{3,0,2,1:T(2,128)(2,1)}), bf16[2,16,12,512]{3,0,2,1:T(2,128)(2,1)S(1)}, u32[]{:S(2)}, u32[]{:S(2)}) async-start(bf16[2,16,12,512]{3,0,2,1:T(2,128)(2,1)} %copy.195), calls=%async_computation.5 | async-start | bytes 786432 | tf_op jit(solution)/shard_map/all_to_all | solution.py:175
  26.9 111.7 %copy-start.4 = (f32[144,512]{1,0:T(8,128)}, f32[144,512]{1,0:T(8,128)S(1)}, u32[]{:S(2)}) copy-start(f32[144,512]{1,0:T(8,128)S(1)} %reshape.688) | copy-start | bytes 884740
  27.1 17.2 %copy-start.19 = (f32[12,12]{1,0:T(8,128)}, f32[12,12]{1,0:T(8,128)S(1)}, u32[]{:S(2)}) copy-start(f32[12,12]{1,0:T(8,128)S(1)} %add_sqrt_fusion) | copy-start | bytes 1732
  27.1 17.1 %copy-start.29 = (f32[144]{0:T(256)}, f32[144]{0:T(256)S(1)}, u32[]{:S(2)}) copy-start(f32[144]{0:T(256)S(1)} %sqrt.13) | copy-start | bytes 1732
  44.3 18.4 %all-to-all-start.1 = ((bf16[2,16,12,512]{3,0,2,1:T(2,128)(2,1)}), bf16[2,16,12,512]{3,0,2,1:T(2,128)(2,1)S(1)}, u32[]{:S(2)}, u32[]{:S(2)}) async-start(bf16[2,16,12,512]{3,0,2,1:T(2,128)(2,1)} %copy.171), calls=%async_computation.1 | async-start | bytes 786432 | tf_op jit(solution)/shard_map/all_to_all | solution.py:174
  50.2 88.4 %copy-start.24 = (s32[144,2]{0,1:T(2,128)}, s32[144,2]{0,1:T(2,128)S(1)}, u32[]{:S(2)}) copy-start(s32[144,2]{0,1:T(2,128)S(1)} %eq.44) | copy-start | bytes 3460
  50.3 88.3 %copy-start.21 = (f32[144,2]{0,1:T(2,128)}, f32[144,2]{0,1:T(2,128)S(1)}, u32[]{:S(2)}) copy-start(f32[144,2]{0,1:T(2,128)S(1)} %select_reduce_fusion.2) | copy-start | bytes 3460
  50.4 88.2 %copy-start.28 = (f32[144]{0:T(256)}, f32[144]{0:T(256)S(1)}, u32[]{:S(2)}) copy-start(f32[144]{0:T(256)S(1)} %reduce_max.28) | copy-start | bytes 1732
  261.8 18.2 %all-to-all-start.4 = ((bf16[2,16,12]{2,0,1:T(2,128)(2,1)}), bf16[2,16,12]{2,0,1:T(2,128)(2,1)}, u32[]{:S(2)}, u32[]{:S(2)}) async-start(bf16[2,16,12]{2,0,1:T(2,128)(2,1)} %copy.197), calls=%async_computation.6 | async-start | bytes 16384 | tf_op jit(solution)/shard_map/all_to_all | solution.py:202
  267.2 273.6 %reduce-scatter.3.cloned.1.call-start = ((), (), s32[]{:S(2)}) async-start(), calls=%async_computation.9 | async-start | bytes 8912896 | tf_op jit(solution)/shard_map/reduce_scatter | solution.py:211
  319.4 5.7 copy-start.12
  325.0 1.2 copy-start
  330.7 1.0 copy-start.13
  330.8 399.1 %reduce-scatter.5.cloned.1.call-start = ((), (), s32[]{:S(2)}) async-start(), calls=%async_computation.10 | async-start | bytes 8912896 | tf_op jit(solution)/shard_map/reduce_scatter | solution.py:212
  336.3 1.1 copy-start.18
  336.3 6.8 copy-start.11
  337.4 19.9 %collective-permute-start = (bf16[3,6,12,512]{3,2,1,0:T(8,128)(2,1)S(1)}, bf16[3,6,12,512]{3,2,1,0:T(8,128)(2,1)S(1)}, u32[]{:S(2)}, u32[]{:S(2)}) collective-permute-start(bf16[3,6,12,512]{3,2,1,0:T(8,128)(2,1)S(1)} %get-tuple-element.24), channel_id=1, source_target_pairs={{1,0},{2,1},{3,2},{4,3},{5,4},{6,5},{7,6},{8,7},{9,8},{10,9},{11,1... | collective-permute-start | bytes 663560 | tf_op jit(solution)/shard_map/ppermute | solution.py:19
  358.6 5.7 copy-start.14
  358.9 5.4 copy-start.1
  368.0 10.9 %copy-start.25 = (s32[144,2]{0,1:T(2,128)S(1)}, s32[144,2]{0,1:T(2,128)}, u32[]{:S(2)}) copy-start(s32[144,2]{0,1:T(2,128)} %copy-done.24) | copy-start | bytes 3460
  368.1 10.9 %copy-start.26 = (f32[144,2]{0,1:T(2,128)S(1)}, f32[144,2]{0,1:T(2,128)}, u32[]{:S(2)}) copy-start(f32[144,2]{0,1:T(2,128)} %convert_element_type.167) | copy-start | bytes 3460
  369.2 25.4 %copy-start.27 = (s32[1024]{0:T(1024)S(1)}, s32[1024]{0:T(1024)}, u32[]{:S(2)}) copy-start(s32[1024]{0:T(1024)} %pad_clamp_fusion) | copy-start | bytes 12292
  369.2 25.2 %all-to-all-start.2 = ((bf16[2,16,12,512]{3,0,2,1:T(2,128)(2,1)}), bf16[2,16,12,512]{3,0,2,1:T(2,128)(2,1)S(1)}, u32[]{:S(2)}, u32[]{:S(2)}) async-start(bf16[2,16,12,512]{3,0,2,1:T(2,128)(2,1)} %bitcast.10), calls=%async_computation.2 | async-start | bytes 786432 | tf_op jit(solution)/shard_map/all_to_all | solution.py:201
  394.5 3.3 copy-start.3
  394.5 3.3 copy-start.20
  394.5 3.6 copy-start.5
  394.5 3.6 copy-start.7
  394.5 3.6 copy-start.30
  397.7 21.6 %copy-start.15 = (bf16[16,144,32]{1,2,0:T(8,128)(2,1)S(1)}, bf16[16,144,32]{1,2,0:T(8,128)(2,1)}, u32[]{:S(2)}) copy-start(bf16[16,144,32]{1,2,0:T(8,128)(2,1)} %copy.176) | copy-start | bytes 442372
  398.3 20.1 %collective-permute-start.1 = (bf16[6,12,512]{2,1,0:T(8,128)(2,1)S(1)}, bf16[6,12,512]{2,1,0:T(8,128)(2,1)S(1)}, u32[]{:S(2)}, u32[]{:S(2)}) collective-permute-start(bf16[6,12,512]{2,1,0:T(8,128)(2,1)S(1)} %slice.78), channel_id=1, source_target_pairs={{1,0},{2,1},{3,2},{4,3},{5,4},{6,5},{7,6},{8,7},{9,8},{10,9},{11,1... | collective-permute-start | bytes 221192 | tf_op jit(solution)/shard_map/ppermute | solution.py:19
  419.4 2.7 copy-start.8
  425.7 2.5 copy-start.9
  427.2 2.6 copy-start.16
  428.7 3.2 copy-start.17
  430.3 19.5 %collective-permute-start.2 = (bf16[3,6,12,512]{3,2,1,0:T(8,128)(2,1)S(1)}, bf16[3,6,12,512]{3,2,1,0:T(8,128)(2,1)S(1)}, u32[]{:S(2)}, u32[]{:S(2)}) collective-permute-start(bf16[3,6,12,512]{3,2,1,0:T(8,128)(2,1)S(1)} %get-tuple-element.14), channel_id=1, source_target_pairs={{15,0},{0,1},{1,2},{2,3},{3,4},{4,5},{5,6},{6,7},{7,8},{8,9},{9,10... | collective-permute-start | bytes 663560 | tf_op jit(solution)/shard_map/ppermute | solution.py:19
Sparse Core Ops, SparseCore 0:
  9.7 128.7 all-gather.4
  140.3 114.0 all-gather.2
  330.9 209.8 reduce-scatter.2
  543.8 186.0 reduce-scatter.4
where the time goes:
time: 739 us; the launch traced here: 736 us
  waiting for transfers between devices  548 us (74%)
  local copies, waits for them, and re-layouts  53.7 us (7%)
  starting transfers between devices  45.5 us (6%)
  matrix products  35.3 us (5%)
  blocking collectives  20.8 us (3%)
  other arithmetic  18 us (2%)
  between operations  14.6 us (2%)
    reduce_scatter x1, waiting for transfers between devices, per_device(): lax.psum_scatter(second_store, 'space', scatter_dimension=2, tiled=True)  189 us
    all_gather x1, waiting for transfers between devices, per_device(): down_piece = lax.all_gather(down_weight, 'space', axis=2, tiled=True)  113 us
    reduce_scatter x1, waiting for transfers between devices, per_device(): lax.psum_scatter(first_store, 'space', scatter_dimension=2, tiled=True)  90.1 us
    all_gather x1, waiting for transfers between devices, per_device(): up_piece = lax.all_gather(up_weight, 'space', axis=2, tiled=True)  75.9 us
    ppermute x3, waiting for transfers between devices, from_behind(): return lax.ppermute(block, axis, route)  40.6 us
    all_to_all x1, blocking collectives, per_device(): lax.all_to_all(send_scaled, 'expert', split_axis=1, concat_axis=1, tiled=...  20.8 us
  transfers between devices with their start and end apart: 11, of which 10 were waited for; matrix products, arithmetic and copies ran while one was open for 9% of the time, Pallas kernels for 0%

commit v1 on v0

--- a/solution.py
+++ b/solution.py
@@ -138,9 +138,11 @@
     scaled_rows = (gate_weight[:, :, None] * cot_rows[:, None, :].astype(jnp.float32)).astype(
         jnp.bfloat16
     )
-    flat_hot = one_hot.reshape(tokens * TOP, EXPERTS).astype(jnp.int32)
-    running = jnp.cumsum(flat_hot, axis=0) - flat_hot
-    slot_index = jnp.sum(running * flat_hot, axis=-1)
+    flat_hot = one_hot.reshape(tokens * TOP, EXPERTS).astype(jnp.float32)
+    choice_pos = jnp.arange(tokens * TOP, dtype=jnp.int32)
+    earlier = (choice_pos[None, :] < choice_pos[:, None]).astype(jnp.bfloat16)
+    running = jnp.dot(earlier, flat_hot.astype(jnp.bfloat16), preferred_element_type=jnp.float32)
+    slot_index = jnp.sum(running * flat_hot, axis=-1).astype(jnp.int32)
     flat_ids = route_ids.reshape(-1)
     destination = (
         flat_ids % local_experts * group_count + flat_ids // local_experts

time: 739 us -> 740 us (level)
  no operation moved by 1% of the time
where the time goes in v1:
time: 740 us; the launch traced here: 738 us
  waiting for transfers between devices  551 us (74%)
  local copies, waits for them, and re-layouts  53.5 us (7%)
  starting transfers between devices  45.4 us (6%)
  matrix products  35.5 us (5%)
  blocking collectives  20.8 us (3%)
  other arithmetic  17 us (2%)
  between operations  14.6 us (2%)
    reduce_scatter x1, waiting for transfers between devices, per_device(): lax.psum_scatter(second_store, 'space', scatter_dimension=2, tiled=True)  189 us
    all_gather x1, waiting for transfers between devices, per_device(): down_piece = lax.all_gather(down_weight, 'space', axis=2, tiled=True)  115 us
    reduce_scatter x1, waiting for transfers between devices, per_device(): lax.psum_scatter(first_store, 'space', scatter_dimension=2, tiled=True)  90.1 us
    all_gather x1, waiting for transfers between devices, per_device(): up_piece = lax.all_gather(up_weight, 'space', axis=2, tiled=True)  73 us
    ppermute x3, waiting for transfers between devices, from_behind(): return lax.ppermute(block, axis, route)  40.7 us
    all_to_all x1, blocking collectives, per_device(): lax.all_to_all(send_scaled, 'expert', split_axis=1, concat_axis=1, tiled=...  20.8 us
  transfers between devices with their start and end apart: 11, of which 10 were waited for; matrix products, arithmetic and copies ran while one was open for 9% of the time, Pallas kernels for 0%

profile of v1, /device:TPU:24, one launch (start us, length us, event | category | flops | bytes accessed | tf_op | source)
XLA Modules:
  0.0 737.8 jit_solution(8884788273180212932)
XLA Ops:
  11.3 1.7 scatter_custom_fusion.2
  14.3 11.5 %all-to-all-start.3 = ((bf16[2,16,12,512]{3,0,2,1:T(2,128)(2,1)}), bf16[2,16,12,512]{3,0,2,1:T(2,128)(2,1)S(1)}, u32[]{:S(2)}, u32[]{:S(2)}) async-start(bf16[2,16,12,512]{3,0,2,1:T(2,128)(2,1)} %copy.187), calls=%async_computation.5 | async-start | bytes 786432 | tf_op jit(solution)/shard_map/all_to_all | solution.py:177
  26.5 1.7 scatter_custom_fusion.1
  29.5 14.3 %all-to-all-done.3 = bf16[2,16,12,512]{3,0,2,1:T(2,128)(2,1)S(1)} async-done(((bf16[2,16,12,512]{3,0,2,1:T(2,128)(2,1)}), bf16[2,16,12,512]{3,0,2,1:T(2,128)(2,1)S(1)}, u32[]{:S(2)}, u32[]{:S(2)}) %all-to-all-start.3) | async-done | bytes 393248 | tf_op jit(solution)/shard_map/all_to_all | solution.py:177
  43.8 5.8 all-to-all-start.1
  51.6 12.5 %all-to-all-done.1 = bf16[2,16,12,512]{3,0,2,1:T(2,128)(2,1)S(1)} async-done(((bf16[2,16,12,512]{3,0,2,1:T(2,128)(2,1)}), bf16[2,16,12,512]{3,0,2,1:T(2,128)(2,1)S(1)}, u32[]{:S(2)}, u32[]{:S(2)}) %all-to-all-start.1) | async-done | bytes 393248 | tf_op jit(solution)/shard_map/all_to_all | solution.py:176
  64.1 73.0 %all-gather.5.cloned.1.call-done = bf16[2,512,2048]{2,1,0:T(8,128)(2,1)} async-done(((bf16[2,512,128]{2,1,0:T(8,128)(2,1)}), bf16[2,512,2048]{2,1,0:T(8,128)(2,1)}) %all-gather.5.cloned.1.call-update) | async-done | bytes 4194320 | tf_op jit(solution)/shard_map/all_gather | solution.py:184
  137.2 3.2 fusion.20
  140.4 115.4 %all-gather.3.cloned.1.call-done = bf16[2,512,2048]{2,1,0:T(8,128)(2,1)} async-done(((bf16[2,512,128]{2,1,0:T(8,128)(2,1)}), bf16[2,512,2048]{2,1,0:T(8,128)(2,1)}) %all-gather.3.cloned.1.call-update) | async-done | bytes 4194320 | tf_op jit(solution)/shard_map/all_gather | solution.py:185
  255.8 4.7 fusion.10
  260.5 1.4 convert_element_type.190
  261.9 1.3 copy.189
  263.2 5.4 all-to-all-start.4
  268.8 1.3 pad_clamp_fusion
  270.1 1.3 sub.117
  271.4 1.4 reduce_sum.142
  274.2 1.4 div.118
  275.5 1.6 convert_element_type.166
  277.2 1.9 mul.197
  279.1 2.3 mul.198
  282.2 2.6 gather_fusion.1
  287.4 1.4 multiply_reduce_fusion.3
  293.7 2.9 scatter_custom_fusion
  296.6 1.9 reshape.662
  298.5 1.4 copy.161
  299.9 20.8 %all_to_all.25 = bf16[2,16,12,512]{3,0,2,1:T(2,128)(2,1)S(1)} all-to-all(bf16[2,16,12,512]{3,0,2,1:T(2,128)(2,1)S(1)} %copy.161), channel_id=1, replica_groups=mesh['expert'=16,'space'=16] {'expert'}, dimensions={1} | all-to-all | bytes 786432 | tf_op jit(solution)/shard_map/all_to_all | solution.py:178
  320.8 5.6 fusion.8
  327.6 4.5 fusion.18
  333.1 4.6 fusion.22
  338.8 5.7 collective-permute-start
  346.1 12.7 %collective-permute-done = bf16[3,6,12,512]{3,2,1,0:T(8,128)(2,1)S(1)} collective-permute-done((bf16[3,6,12,512]{3,2,1,0:T(8,128)(2,1)S(1)}, bf16[3,6,12,512]{3,2,1,0:T(8,128)(2,1)S(1)}, u32[]{:S(2)}, u32[]{:S(2)}) %collective-permute-start) | collective-permute-done | bytes 221216 | tf_op jit(solution)/shard_map/ppermute | solution.py:19
  361.2 1.2 copy.168
  362.4 3.3 fusion.55
  365.7 3.8 convolution_convert_fusion
  370.6 7.9 %all-to-all-start.2 = ((bf16[2,16,12,512]{3,0,2,1:T(2,128)(2,1)}), bf16[2,16,12,512]{3,0,2,1:T(2,128)(2,1)S(1)}, u32[]{:S(2)}, u32[]{:S(2)}) async-start(bf16[2,16,12,512]{3,0,2,1:T(2,128)(2,1)} %bitcast.9), calls=%async_computation.2 | async-start | bytes 786432 | tf_op jit(solution)/shard_map/all_to_all | solution.py:203
  378.5 1.9 fusion.17
  381.5 14.4 %all-to-all-done.2 = bf16[2,16,12,512]{3,0,2,1:T(2,128)(2,1)S(1)} async-done(((bf16[2,16,12,512]{3,0,2,1:T(2,128)(2,1)}), bf16[2,16,12,512]{3,0,2,1:T(2,128)(2,1)S(1)}, u32[]{:S(2)}, u32[]{:S(2)}) %all-to-all-start.2) | async-done | bytes 393248 | tf_op jit(solution)/shard_map/all_to_all | solution.py:203
  396.0 2.0 gather_fusion
  399.7 7.2 collective-permute-start.1
  408.7 11.1 %collective-permute-done.1 = bf16[6,12,512]{2,1,0:T(8,128)(2,1)S(1)} collective-permute-done((bf16[6,12,512]{2,1,0:T(8,128)(2,1)S(1)}, bf16[6,12,512]{2,1,0:T(8,128)(2,1)S(1)}, u32[]{:S(2)}, u32[]{:S(2)}) %collective-permute-start.1) | collective-permute-done | bytes 73760 | tf_op jit(solution)/shard_map/ppermute | solution.py:19
  421.1 2.4 multiply_convert_fusion.1
  424.5 1.4 copy.175
  425.9 1.2 stack_reshape.9
  427.1 1.5 fusion.11
  431.6 1.7 collective-permute-start.2
  434.2 16.9 %collective-permute-done.2 = bf16[3,6,12,512]{3,2,1,0:T(8,128)(2,1)S(1)} collective-permute-done((bf16[3,6,12,512]{3,2,1,0:T(8,128)(2,1)S(1)}, bf16[3,6,12,512]{3,2,1,0:T(8,128)(2,1)S(1)}, u32[]{:S(2)}, u32[]{:S(2)}) %collective-permute-start.2) | collective-permute-done | bytes 221216 | tf_op jit(solution)/shard_map/ppermute | solution.py:19
  452.0 90.1 %reduce-scatter.3.cloned.1.call-done = f32[2,512,128]{2,1,0:T(8,128)} async-done(((f32[2,512,2048]{2,1,0:T(8,128)}), f32[2,512,128]{2,1,0:T(8,128)}) %reduce-scatter.3.cloned.1.call-update) | async-done | bytes 524304 | tf_op jit(solution)/shard_map/reduce_scatter | solution.py:213
  542.2 189.1 %reduce-scatter.5.cloned.1.call-done = f32[2,512,128]{2,1,0:T(8,128)} async-done(((f32[2,512,2048]{2,1,0:T(8,128)}), f32[2,512,128]{2,1,0:T(8,128)}) %reduce-scatter.5.cloned.1.call-update) | async-done | bytes 524304 | tf_op jit(solution)/shard_map/reduce_scatter | solution.py:214
  (171 shorter events, 39.0 us)
Async XLA Ops:
  7.2 18.6 %copy-start.2 = (bf16[1,12,12,512]{3,2,1,0:T(8,128)(2,1)S(1)}, bf16[1,12,12,512]{3,2,1,0:T(8,128)(2,1)}, u32[]{:S(2)}) copy-start(bf16[1,12,12,512]{3,2,1,0:T(8,128)(2,1)} %param.9) | copy-start | bytes 442372
  7.2 130.0 %all-gather.5.cloned.1.call-start = ((), (), s32[]{:S(2)}) async-start(), calls=%async_computation.8 | async-start | bytes 4456448 | tf_op jit(solution)/shard_map/all_gather | solution.py:184
  7.9 247.9 %all-gather.3.cloned.1.call-start = ((), (), s32[]{:S(2)}) async-start(), calls=%async_computation.7 | async-start | bytes 4456448 | tf_op jit(solution)/shard_map/all_gather | solution.py:185
  11.0 17.2 %copy-start.6 = (bf16[144,512]{1,0:T(8,128)(2,1)}, bf16[144,512]{1,0:T(8,128)(2,1)S(1)}, u32[]{:S(2)}) copy-start(bf16[144,512]{1,0:T(8,128)(2,1)S(1)} %reshape_squeeze.17) | copy-start | bytes 442372
  11.3 17.0 %copy-start.31 = (s32[288]{0:T(512)}, s32[288]{0:T(512)S(1)}, u32[]{:S(2)}) copy-start(s32[288]{0:T(512)S(1)} %fusion.41) | copy-start | bytes 3460
  14.3 35.3 %copy-start.22 = (s32[1,12,12,2]{2,3,1,0:T(2,128)S(1)}, s32[1,12,12,2]{2,3,1,0:T(2,128)}, u32[]{:S(2)}) copy-start(s32[1,12,12,2]{2,3,1,0:T(2,128)} %param.11) | copy-start | bytes 3460
  14.3 35.4 %copy-start.10 = (f32[1,12,12,32]{3,0,2,1:T(1,128)S(1)}, f32[1,12,12,32]{3,0,2,1:T(1,128)}, u32[]{:S(2)}) copy-start(f32[1,12,12,32]{3,0,2,1:T(1,128)} %param.10) | copy-start | bytes 55300
  14.3 36.1 %copy-start.23 = (s32[1,12,12,2]{2,3,1,0:T(2,128)S(1)}, s32[1,12,12,2]{2,3,1,0:T(2,128)}, u32[]{:S(2)}) copy-start(s32[1,12,12,2]{2,3,1,0:T(2,128)} %param.12) | copy-start | bytes 3460
  14.3 29.4 %all-to-all-start.3 = ((bf16[2,16,12,512]{3,0,2,1:T(2,128)(2,1)}), bf16[2,16,12,512]{3,0,2,1:T(2,128)(2,1)S(1)}, u32[]{:S(2)}, u32[]{:S(2)}) async-start(bf16[2,16,12,512]{3,0,2,1:T(2,128)(2,1)} %copy.187), calls=%async_computation.5 | async-start | bytes 786432 | tf_op jit(solution)/shard_map/all_to_all | solution.py:177
  25.8 111.3 %copy-start.4 = (f32[144,512]{1,0:T(8,128)}, f32[144,512]{1,0:T(8,128)S(1)}, u32[]{:S(2)}) copy-start(f32[144,512]{1,0:T(8,128)S(1)} %reshape.678) | copy-start | bytes 884740
  26.0 17.8 %copy-start.19 = (f32[12,12]{1,0:T(8,128)}, f32[12,12]{1,0:T(8,128)S(1)}, u32[]{:S(2)}) copy-start(f32[12,12]{1,0:T(8,128)S(1)} %add_sqrt_fusion) | copy-start | bytes 1732
  26.1 17.7 %copy-start.29 = (f32[144]{0:T(256)}, f32[144]{0:T(256)S(1)}, u32[]{:S(2)}) copy-start(f32[144]{0:T(256)S(1)} %sqrt.13) | copy-start | bytes 1732
  43.8 20.4 %all-to-all-start.1 = ((bf16[2,16,12,512]{3,0,2,1:T(2,128)(2,1)}), bf16[2,16,12,512]{3,0,2,1:T(2,128)(2,1)S(1)}, u32[]{:S(2)}, u32[]{:S(2)}) async-start(bf16[2,16,12,512]{3,0,2,1:T(2,128)(2,1)} %copy.163), calls=%async_computation.1 | async-start | bytes 786432 | tf_op jit(solution)/shard_map/all_to_all | solution.py:176
  49.7 87.5 %copy-start.24 = (s32[144,2]{0,1:T(2,128)}, s32[144,2]{0,1:T(2,128)S(1)}, u32[]{:S(2)}) copy-start(s32[144,2]{0,1:T(2,128)S(1)} %eq.34) | copy-start | bytes 3460
  49.8 87.4 %copy-start.21 = (f32[144,2]{0,1:T(2,128)}, f32[144,2]{0,1:T(2,128)S(1)}, u32[]{:S(2)}) copy-start(f32[144,2]{0,1:T(2,128)S(1)} %select_reduce_fusion.2) | copy-start | bytes 3460
  49.8 87.3 %copy-start.28 = (f32[144]{0:T(256)}, f32[144]{0:T(256)S(1)}, u32[]{:S(2)}) copy-start(f32[144]{0:T(256)S(1)} %reduce_max.28) | copy-start | bytes 1732
  263.2 18.2 %all-to-all-start.4 = ((bf16[2,16,12]{2,0,1:T(2,128)(2,1)}), bf16[2,16,12]{2,0,1:T(2,128)(2,1)}, u32[]{:S(2)}, u32[]{:S(2)}) async-start(bf16[2,16,12]{2,0,1:T(2,128)(2,1)} %copy.189), calls=%async_computation.6 | async-start | bytes 16384 | tf_op jit(solution)/shard_map/all_to_all | solution.py:204
  268.6 273.6 %reduce-scatter.3.cloned.1.call-start = ((), (), s32[]{:S(2)}) async-start(), calls=%async_computation.9 | async-start | bytes 8912896 | tf_op jit(solution)/shard_map/reduce_scatter | solution.py:213
  320.8 5.7 copy-start.12
  326.4 1.2 copy-start
  332.1 1.0 copy-start.13
  332.1 399.1 %reduce-scatter.5.cloned.1.call-start = ((), (), s32[]{:S(2)}) async-start(), calls=%async_computation.10 | async-start | bytes 8912896 | tf_op jit(solution)/shard_map/reduce_scatter | solution.py:214
  337.7 1.1 copy-start.18
  337.7 6.8 copy-start.11
  338.8 19.9 %collective-permute-start = (bf16[3,6,12,512]{3,2,1,0:T(8,128)(2,1)S(1)}, bf16[3,6,12,512]{3,2,1,0:T(8,128)(2,1)S(1)}, u32[]{:S(2)}, u32[]{:S(2)}) collective-permute-start(bf16[3,6,12,512]{3,2,1,0:T(8,128)(2,1)S(1)} %get-tuple-element.24), channel_id=1, source_target_pairs={{1,0},{2,1},{3,2},{4,3},{5,4},{6,5},{7,6},{8,7},{9,8},{10,9},{11,1... | collective-permute-start | bytes 663560 | tf_op jit(solution)/shard_map/ppermute | solution.py:19
  360.0 5.7 copy-start.14
  360.3 5.4 copy-start.1
  369.4 10.9 %copy-start.25 = (s32[144,2]{0,1:T(2,128)S(1)}, s32[144,2]{0,1:T(2,128)}, u32[]{:S(2)}) copy-start(s32[144,2]{0,1:T(2,128)} %copy-done.24) | copy-start | bytes 3460
  369.5 10.9 %copy-start.26 = (f32[144,2]{0,1:T(2,128)S(1)}, f32[144,2]{0,1:T(2,128)}, u32[]{:S(2)}) copy-start(f32[144,2]{0,1:T(2,128)} %convert_element_type.186) | copy-start | bytes 3460
  370.6 25.4 %copy-start.27 = (s32[1024]{0:T(1024)S(1)}, s32[1024]{0:T(1024)}, u32[]{:S(2)}) copy-start(s32[1024]{0:T(1024)} %pad_clamp_fusion) | copy-start | bytes 12292
  370.6 25.2 %all-to-all-start.2 = ((bf16[2,16,12,512]{3,0,2,1:T(2,128)(2,1)}), bf16[2,16,12,512]{3,0,2,1:T(2,128)(2,1)S(1)}, u32[]{:S(2)}, u32[]{:S(2)}) async-start(bf16[2,16,12,512]{3,0,2,1:T(2,128)(2,1)} %bitcast.9), calls=%async_computation.2 | async-start | bytes 786432 | tf_op jit(solution)/shard_map/all_to_all | solution.py:203
  395.9 3.3 copy-start.3
  395.9 3.3 copy-start.20
  395.9 3.6 copy-start.5
  395.9 3.6 copy-start.7
  395.9 3.6 copy-start.30
  399.1 21.6 %copy-start.15 = (bf16[16,144,32]{1,2,0:T(8,128)(2,1)S(1)}, bf16[16,144,32]{1,2,0:T(8,128)(2,1)}, u32[]{:S(2)}) copy-start(bf16[16,144,32]{1,2,0:T(8,128)(2,1)} %copy.168) | copy-start | bytes 442372
  399.7 20.0 %collective-permute-start.1 = (bf16[6,12,512]{2,1,0:T(8,128)(2,1)S(1)}, bf16[6,12,512]{2,1,0:T(8,128)(2,1)S(1)}, u32[]{:S(2)}, u32[]{:S(2)}) collective-permute-start(bf16[6,12,512]{2,1,0:T(8,128)(2,1)S(1)} %slice.66), channel_id=1, source_target_pairs={{1,0},{2,1},{3,2},{4,3},{5,4},{6,5},{7,6},{8,7},{9,8},{10,9},{11,1... | collective-permute-start | bytes 221192 | tf_op jit(solution)/shard_map/ppermute | solution.py:19
  420.8 2.7 copy-start.8
  427.1 2.5 copy-start.9
  428.6 2.6 copy-start.16
  430.1 3.2 copy-start.17
  431.6 19.5 %collective-permute-start.2 = (bf16[3,6,12,512]{3,2,1,0:T(8,128)(2,1)S(1)}, bf16[3,6,12,512]{3,2,1,0:T(8,128)(2,1)S(1)}, u32[]{:S(2)}, u32[]{:S(2)}) collective-permute-start(bf16[3,6,12,512]{3,2,1,0:T(8,128)(2,1)S(1)} %get-tuple-element.14), channel_id=1, source_target_pairs={{15,0},{0,1},{1,2},{2,3},{3,4},{4,5},{5,6},{6,7},{7,8},{8,9},{9,10... | collective-permute-start | bytes 663560 | tf_op jit(solution)/shard_map/ppermute | solution.py:19
Sparse Core Ops, SparseCore 0:
  9.7 127.3 all-gather.4
  138.9 116.8 all-gather.2
  332.3 209.8 reduce-scatter.2
  545.2 186.0 reduce-scatter.4

commit v2 on v0

v2 whole, which is shorter than its diff:
```python
import jax
import jax.numpy as jnp
from jax import lax
from jax.experimental import pallas as pl
from jax.experimental.pallas import tpu as pltpu
from jax.sharding import PartitionSpec as P

WIN = 12
PADW = 16
TOK = WIN * PADW
HALF = TOK // 2
C = 512
HEADS = 16
EXPERTS = 32
CAP = 12
NE = 16
NX = 4
NZ = 4
HID = 128
NORM_EPS = 1e-06
SCORE_MASK = -100.0
NO_KEY = -1e30
GELU_C = 0.7978845608028654
GELU_A = 0.044715
F32 = jnp.float32
BF16 = jnp.bfloat16
I32 = jnp.int32


def iota(shape, dim):
    return lax.broadcasted_iota(I32, shape, dim)


def dot(a, b):
    return lax.dot_general(a, b, (((1,), (0,)), ((), ())), preferred_element_type=F32)


def dot_nt(a, b):
    return lax.dot_general(a, b, (((1,), (1,)), ((), ())), preferred_element_type=F32)


def dot_tn(a, b):
    return lax.dot_general(a, b, (((0,), (0,)), ((), ())), preferred_element_type=F32)


def ge(a, n):
    return (a >= n).astype(I32)


def ones_where(cond):
    return jnp.where(cond, 1.0, 0.0).astype(BF16)


def split_tail(x):
    total = x[96:97] + x[97:98]
    high = total.astype(BF16).astype(F32)
    low = total - high
    row = iota((16, C), 0)
    tail = jnp.where(row == 0, high, jnp.where(row == 1, low, 0.0))
    return jnp.concatenate([x[:96], tail], axis=0).astype(BF16)


def kernel(
    attn_ref, resid_ref, logit_ref, ids_ref, keep_ref, cot_ref, up_ref, down_ref,
    attn_out, res_out, up_out, down_out, logit_out,
    qw, qsend, gw, gsend, agrad, asend, arecv,
    resid_s, cot_s, lg_s, ids_s, keep_s, cols, stage, probs, perm_s, bias_s,
    send_rows, recv_rows, rows_all, w_all, wcat, pg_s, act_s, part, xs, xr,
    ret_send, ret_recv, grads, zsend, zrecv,
    d_ss, d_rs, g_ss, g_rs, w_ss, w_rs, x_ss, x_rs, r_ss, r_rs, z_ss, z_rs, h_ss, h_rs,
):
    me_e = lax.axis_index("expert")
    me_s = lax.axis_index("space")
    mx = me_s // NZ
    mz = me_s % NZ
    zhi = me_e // 8
    x1 = mx + 1 - 2 * (mx % 2)
    x3 = NX - 1 - mx
    x2 = NX - 1 - x1
    z1 = mz + 1 - 2 * (mz % 2)
    z3 = NZ - 1 - mz
    z2 = NZ - 1 - z1
    dev_x1 = x1 * NZ + mz
    dev_x3 = x3 * NZ + mz
    dev_z1 = mx * NZ + z1
    dev_z2 = mx * NZ + z2
    after = (me_s + 1) % (NX * NZ)
    before = (me_s + NX * NZ - 1) % (NX * NZ)

    def remote(src, dst, ss, rs, e, s):
        return pltpu.make_async_remote_copy(
            src_ref=src, dst_ref=dst, send_sem=ss, recv_sem=rs,
            device_id={"expert": e, "space": s}, device_id_type=pl.DeviceIdType.MESH,
        )

    barrier = pltpu.get_barrier_semaphore()

    def greet(e, s):
        pl.semaphore_signal(
            barrier, inc=1, device_id={"expert": e, "space": s}, device_id_type=pl.DeviceIdType.MESH
        )

    @pl.loop(1, NE)
    def _(i):
        greet((me_e + i) % NE, me_s)

    for s in (dev_x1, dev_x3, dev_z1, dev_z2, after, before):
        greet(me_e, s)

    half_rows = WIN // 2
    qw[0] = jnp.zeros((3, HALF, C), BF16)
    qsend[...] = jnp.zeros((3, HALF, C), BF16)
    resid_s[...] = jnp.zeros((TOK, C), BF16)
    cot_s[...] = jnp.zeros((TOK, C), BF16)
    lg_s[...] = jnp.zeros((TOK, EXPERTS), F32)
    ids_s[...] = jnp.full((TOK, 2), -1, I32)
    keep_s[...] = jnp.zeros((TOK, 2), I32)
    for r in range(WIN):
        at = pl.ds(r * PADW, WIN)
        resid_s[at, :] = resid_ref[r]
        cot_s[at, :] = cot_ref[r]
        lg_s[at, :] = logit_ref[r]
        ids_s[at, :] = ids_ref[r]
        keep_s[at, :] = keep_ref[r]
    for r in range(half_rows):
        for k in range(3):
            qsend[k, pl.ds(r * PADW, WIN), :] = attn_ref[k, r]
            qw[0, k, pl.ds(r * PADW, WIN), :] = attn_ref[k, half_rows + r]

    pl.semaphore_wait(barrier, NE - 1 + 6)

    own_w = []
    for m, ref in ((0, up_ref), (1, down_ref)):
        own_w.append(remote(ref, w_all.at[mz, m], w_ss.at[0, m], w_rs.at[0, m], me_e, dev_z2))
    for m, ref in ((0, up_ref), (1, down_ref)):
        own_w.append(remote(ref, w_all.at[mz, m], w_ss.at[1, m], w_rs.at[1, m], me_e, dev_z1))
    halo_q = remote(qsend, qw.at[1], h_ss.at[0], h_rs.at[0], me_e, before)

    resid = resid_s[...].astype(F32)
    rms = jnp.sqrt(jnp.mean(resid * resid, axis=-1, keepdims=True) + NORM_EPS)
    nf = resid / rms
    normed = nf.astype(BF16)
    cot = cot_s[...].astype(F32)
    lg = lg_s[...]
    ids = ids_s[...]
    keep = keep_s[...].astype(F32)
    id1, id2 = ids[:, 0:1], ids[:, 1:2]
    keep1, keep2 = keep[:, 0:1], keep[:, 1:2]
    expert = iota((TOK, EXPERTS), 1)
    oh1 = jnp.where(expert == id1, 1.0, 0.0)
    oh2 = jnp.where(expert == id2, 1.0, 0.0)
    l1 = jnp.sum(jnp.where(expert == id1, lg, 0.0), axis=-1, keepdims=True)
    l2 = jnp.sum(jnp.where(expert == id2, lg, 0.0), axis=-1, keepdims=True)
    lm = jnp.maximum(l1, l2)
    e1, e2 = jnp.exp(l1 - lm), jnp.exp(l2 - lm)
    gate1, gate2 = e1 / (e1 + e2), e2 / (e1 + e2)
    scaled1 = (gate1 * keep1 * cot).astype(BF16)
    scaled2 = (gate2 * keep2 * cot).astype(BF16)
    square_r, square_c = iota((TOK, TOK), 0), iota((TOK, TOK), 1)
    counts = dot(ones_where(square_c < square_r), (oh1 + oh2).astype(BF16))
    slot1 = jnp.sum(oh1 * counts, axis=-1, keepdims=True).astype(I32)
    slot2 = jnp.sum(oh2 * counts, axis=-1, keepdims=True).astype(I32)
    q1 = id1 * CAP + slot1
    q2 = id2 * CAP + slot2
    q1_row = jnp.sum(jnp.where(square_r == square_c, q1, 0), axis=0, keepdims=True)
    q2_row = jnp.sum(jnp.where(square_r == square_c, q2, 0), axis=0, keepdims=True)
    lane = iota((TOK, 128), 1)
    column = jnp.zeros((TOK, 128), F32)
    for i, v in enumerate((gate1, gate2, rms, keep1, keep2)):
        column = jnp.where(lane == i, v, column)
    cols[...] = column

    row = iota((TOK, 1), 0)
    src4 = ge(row, 48) + ge(row, 96) + ge(row, 144)
    rem = row - 48 * src4
    second = ge(rem, 24)

    @pl.loop(0, 4)
    def _(k):
        ch = (2 * (1 - zhi) + k) % 4
        q = (ch * 4 + src4) * 24 + rem - 24 * second
        m1 = q == q1_row
        m2 = q == q2_row
        is_norm = second == 0
        pn = ones_where((m1 | m2) & is_norm)
        ps1 = ones_where(m1 & (second == 1))
        ps2 = ones_where(m2 & (second == 1))
        built = dot(pn, normed) + dot(ps1, scaled1) + dot(ps2, scaled2)
        send_rows[pl.ds(ch * 4, 4)] = built.astype(BF16).reshape(4, 48, C)
        for s in range(4):
            to = ch * 4 + s

            @pl.when(to != me_e)
            def _():
                remote(
                    send_rows.at[to], recv_rows.at[me_e], d_ss.at[to], d_rs.at[me_e], to, me_s
                ).start()

    for cp in own_w:
        cp.start()
    halo_q.start()
    recv_rows[me_e] = send_rows[me_e]

    b96 = ge(row, 96)
    o2 = row - 96 * b96
    b48 = ge(o2, 48)
    o3 = o2 - 48 * b48
    s12 = ge(o3, 12) + ge(o3, 24) + ge(o3, 36)
    perm_s[...] = ones_where(square_c == s12 * 48 + b96 * 24 + b48 * 12 + (o3 - 12 * s12))

    pos_r = square_r % PADW
    pos_c = square_c % PADW
    differ = (pos_r >= half_rows) != (pos_c >= half_rows)
    is_last = me_s == NX * NZ - 1
    last_i = jnp.where(is_last, 1, 0)
    half_differ = (ge(square_r, HALF) != ge(square_c, HALF)) & ((square_r * 0 + last_i) == 1)
    bias = jnp.where(differ | half_differ, SCORE_MASK, 0.0)
    bias_s[...] = jnp.where(pos_c >= WIN, NO_KEY, bias)
    inv_sqrt = (C // HEADS) ** (-0.5)
    halo_q.wait_recv()

    head_lane = iota((1, 128), 1)

    def head_mask(h):
        return ones_where((head_lane >= h * 32) & (head_lane < (h + 1) * 32))

    @pl.loop(0, 4)
    def _(lg_i):
        lanes = pl.ds(pl.multiple_of(lg_i * 128, 128), 128)
        q = jnp.concatenate([qw[0, 0, :, lanes], qw[1, 0, :, lanes]], axis=0)
        k = jnp.concatenate([qw[0, 1, :, lanes], qw[1, 1, :, lanes]], axis=0)
        for h in range(4):
            sc = dot_nt(q * head_mask(h), k) * inv_sqrt + bias_s[...]
            ex = jnp.exp(sc - jnp.max(sc, axis=-1, keepdims=True))
            probs[lg_i * 4 + h] = ex / jnp.sum(ex, axis=-1, keepdims=True)

    @pl.loop(0, 4)
    def _(k):
        grp = (2 * zhi + k) % 4
        for s in range(4):
            frm = grp * 4 + s

            @pl.when(frm != me_e)
            def _():
                remote(
                    send_rows.at[frm], recv_rows.at[frm], d_ss.at[frm], d_rs.at[frm], frm, me_s
                ).wait()

        block = recv_rows[pl.ds(grp * 4, 4)].reshape(TOK, C)
        rows_all[mx, grp] = dot(perm_s[...], block).astype(BF16).reshape(2, 2, 48, C)
        remote(
            rows_all.at[mx, grp], rows_all.at[mx, grp], g_ss.at[0, grp], g_rs.at[0, grp], me_e, dev_x1
        ).start()
        remote(
            rows_all.at[mx, grp], rows_all.at[mx, grp], g_ss.at[1, grp], g_rs.at[1, grp], me_e, dev_x3
        ).start()

    fwd_w = []
    for m in range(2):
        own_w[m].wait_recv()
        cp = remote(
            w_all.at[z2, m], w_all.at[z2, m], w_ss.at[2, m], w_rs.at[2, m], me_e, dev_z1
        )
        cp.start()
        fwd_w.append(cp)

    def x_recv(which, grp):
        frm, dev = ((x1, dev_x1), (x3, dev_x3))[which]
        return remote(
            rows_all.at[frm, grp], rows_all.at[frm, grp], g_ss.at[which, grp], g_rs.at[which, grp],
            me_e, dev,
        )

    fwd_x = []
    for grp in range(4):
        which = 0 if grp < 2 else 1
        x_recv(which, grp).wait_recv()
        frm, dev = ((x1, dev_x3), (x3, dev_x1))[which]
        cp = remote(
            rows_all.at[frm, grp], rows_all.at[frm, grp], g_ss.at[2, grp], g_rs.at[2, grp], me_e, dev
        )
        cp.start()
        fwd_x.append(cp)

    for m in range(2):
        own_w[2 + m].wait_recv()
        fwd_w[m].wait_recv()
    w_all[mz, 0] = up_ref[...]
    w_all[mz, 1] = down_ref[...]
    for m in range(2):
        for j in range(2):
            wcat[m, j] = jnp.concatenate([w_all[c, m, j] for c in range(NZ)], axis=1)

    def expert_rows(b):
        for j in range(2):
            xn = rows_all[b, :, 0, j].reshape(192, C)
            xsc = rows_all[b, :, 1, j].reshape(192, C)
            pre = dot(xn, wcat[0, j])
            sq = pre * pre
            t = jnp.tanh(GELU_C * pre * (1.0 + GELU_A * sq))
            act = (0.5 * pre * (1.0 + t)).astype(BF16)
            slope = 0.5 * (1.0 + t) + 0.5 * GELU_C * pre * (1.0 - t * t) * (1.0 + 3.0 * GELU_A * sq)
            dact = dot(xsc, wcat[1, j])
            dsum = jnp.sum(act.astype(F32) * dact, axis=-1, keepdims=True)
            pg = (dact * slope).astype(BF16)
            act_s[b, j] = act
            pg_s[b, j] = pg
            rg = dot_nt(pg, wcat[0, j])
            part[b, :, pl.ds(j * 48, 48), :] = rg.reshape(4, 48, C)
            hit = iota((48, C), 1) == iota((48, C), 0) + j * 48
            for g in range(4):
                line = jnp.sum(
                    jnp.where(hit, dsum[g * 48 : (g + 1) * 48], 0.0), axis=0, keepdims=True
                )
                if j == 0:
                    tail = jnp.where(iota((16, C), 0) == 0, line, 0.0)
                    part[b, g, pl.ds(96, 16), :] = tail
                else:
                    tail = jnp.where(iota((16, C), 0) == 0, line, 0.0)
                    part[b, g, pl.ds(96, 16), :] += tail

    def x_send(n, dev, slot, sem):
        return remote(xs.at[n], xr.at[slot], x_ss.at[n], x_rs.at[sem], me_e, dev)

    expert_rows(mx)
    x_recv(0, 2).wait_recv()
    x_recv(0, 3).wait_recv()
    expert_rows(x1)
    sums = []
    for g in (0, 1):
        xs[g] = split_tail(part[x1, g])
        sums.append(x_send(g, dev_x1, g, g))
        sums[-1].start()
    x_recv(1, 0).wait_recv()
    x_recv(1, 1).wait_recv()
    expert_rows(x3)
    for g in (2, 3):
        xs[4 + g] = split_tail(part[x3, g])
        sums.append(x_send(4 + g, dev_x3, 4 + g, 4 + g))
        sums[-1].start()
    for cp in fwd_x:
        cp.wait_recv()
    expert_rows(x2)
    for g in (0, 1):
        xs[8 + g] = split_tail(part[x2, g])
        sums.append(x_send(8 + g, dev_x1, 8 + g, 8 + g))
        sums[-1].start()
    for g in (2, 3):
        xs[8 + g] = split_tail(part[x2, g])
        sums.append(x_send(8 + g, dev_x3, 8 + g, 8 + g))
        sums[-1].start()

    def x_got(slot):
        return remote(xs.at[slot], xr.at[slot], x_ss.at[slot], x_rs.at[slot], me_e, dev_x1)

    zsent = []

    def weight_grad(m, j):
        left = rows_all[:, :, m, j].reshape(4 * 192, C)
        right = (pg_s, act_s)[m][:, j].reshape(4 * 192, C)
        full = dot_tn(left, right)
        for c in range(NZ):
            grads[m, j, c] = full[:, c * HID : (c + 1) * HID]
        zsend[0, m, j] = grads[m, j, z3].astype(BF16)
        zsend[1, m, j] = grads[m, j, z1].astype(BF16)
        for n in range(2):
            cp = remote(
                zsend.at[n, m, j], zrecv.at[n, m, j], z_ss.at[n, m, j], z_rs.at[n, m, j], me_e, dev_z1
            )
            cp.start()
            zsent.append(cp)

    def z_forward(m, j):
        zsent[2 * (2 * m + j)].wait_recv()
        zsend[2, m, j] = (grads[m, j, z2] + zrecv[0, m, j].astype(F32)).astype(BF16)
        cp = remote(
            zsend.at[2, m, j], zrecv.at[2, m, j], z_ss.at[2, m, j], z_rs.at[2, m, j], me_e, dev_z2
        )
        cp.start()
        zlast.append(cp)

    zlast = []
    weight_grad(0, 0)
    weight_grad(0, 1)
    for g in (0, 1):
        x_got(8 + g).wait_recv()
        xs[4 + g] = split_tail(part[x3, g] + xr[8 + g].astype(F32))
        sums.append(x_send(4 + g, dev_x3, 4 + g, 4 + g))
        sums[-1].start()
    for g in (2, 3):
        x_got(8 + g).wait_recv()
        xs[g] = split_tail(part[x1, g] + xr[8 + g].astype(F32))
        sums.append(x_send(g, dev_x1, g, g))
        sums[-1].start()
    weight_grad(1, 0)
    weight_grad(1, 1)

    ro = iota((128, 112), 0)
    rs = ge(ro, 32) + ge(ro, 64) + ge(ro, 96)
    rq = ro - 32 * rs
    rj = ge(rq, 12)
    want = jnp.where(rq < 24, rj * 48 + rs * 12 + rq - 12 * rj, jnp.where(rq < 26, rq + 72, -1))
    back = ones_where(iota((128, 112), 1) == want)
    for g in range(4):
        x_got(g).wait_recv()
        x_got(4 + g).wait_recv()
        total = split_tail(part[mx, g] + xr[g].astype(F32) + xr[4 + g].astype(F32))
        ret_send[pl.ds(g * 4, 4)] = dot(back, total).astype(BF16).reshape(4, 32, C)
        for s in range(4):
            to = g * 4 + s

            @pl.when(to != me_e)
            def _():
                remote(
                    ret_send.at[to], ret_recv.at[me_e], r_ss.at[to], r_rs.at[me_e], to, me_s
                ).start()

    ret_recv[me_e] = ret_send[me_e]
    for m in range(2):
        for j in range(2):
            z_forward(m, j)

    @pl.loop(0, NE)
    def _(frm):
        @pl.when(frm != me_e)
        def _():
            remote(
                ret_send.at[frm], ret_recv.at[frm], r_ss.at[frm], r_rs.at[frm], frm, me_s
            ).wait()

    returned = ret_recv[...].reshape(NE * 32, C)
    ids = ids_s[...]
    id1, id2 = ids[:, 0:1], ids[:, 1:2]
    expert = iota((TOK, EXPERTS), 1)
    hot1, hot2 = expert == id1, expert == id2
    oh1, oh2 = jnp.where(hot1, 1.0, 0.0), jnp.where(hot2, 1.0, 0.0)
    counts = dot(ones_where(square_c < square_r), (oh1 + oh2).astype(BF16))
    slot1 = jnp.sum(oh1 * counts, axis=-1, keepdims=True).astype(I32)
    slot2 = jnp.sum(oh2 * counts, axis=-1, keepdims=True).astype(I32)
    q1 = id1 * CAP + slot1
    q2 = id2 * CAP + slot2
    col = iota((TOK, NE * 32), 1)
    dev = lax.shift_right_arithmetic(col, 5)
    pos = col - 32 * dev
    at = dev * 24 + pos
    pick = ones_where(((at == q1) | (at == q2)) & (pos < 24))
    norm_grad = dot(pick, returned)
    rms = cols[:, 2:3]
    resid = resid_s[...].astype(F32)
    nf = resid / rms
    inner = jnp.mean(norm_grad * nf, axis=-1, keepdims=True)
    cot = cot_s[...].astype(F32)
    res_grad = (cot + (norm_grad - nf * inner) / rms).astype(BF16)
    stage[...] = res_grad
    gsend[...] = stage[pl.ds(0, HALF), :]
    halo_g = remote(gsend, gw.at[1], h_ss.at[1], h_rs.at[1], me_e, before)
    halo_g.start()
    gw[0] = stage[pl.ds(HALF, HALF), :]
    for r in range(WIN):
        res_out[r] = stage[pl.ds(r * PADW, WIN), :]

    gate1, gate2 = cols[:, 0:1], cols[:, 1:2]
    keep1, keep2 = cols[:, 3:4], cols[:, 4:5]
    narrow = returned[:, :128]
    tail_pos = (pos == 24) | (pos == 25)

    def gathered(idk, slotk):
        half = lax.shift_right_arithmetic(idk, 1)
        pickk = ones_where((dev == half) & tail_pos)
        found = dot(pickk, narrow)
        spot = (idk - 2 * half) * 48 + (me_e % 4) * 12 + slotk
        return jnp.sum(jnp.where(iota((TOK, 128), 1) == spot, found, 0.0), axis=-1, keepdims=True)

    d1 = gathered(id1, slot1)
    d2 = gathered(id2, slot2)
    part1 = gate2 * d1 - gate1 * d2
    share = jnp.sum(oh1 * keep1 + oh2 * keep2, axis=0, keepdims=True) / (2.0 * WIN * WIN)
    lg = lg_s[...]
    lex = jnp.exp(lg - jnp.max(lg, axis=-1, keepdims=True))
    rp = lex / jnp.sum(lex, axis=-1, keepdims=True)
    share_mean = jnp.sum(rp * share, axis=-1, keepdims=True)
    lg_s[...] = (oh1 - oh2) * part1 + EXPERTS * rp * (share - share_mean)
    for r in range(WIN):
        logit_out[r] = lg_s[pl.ds(r * PADW, WIN), :]

    halo_g.wait_recv()

    @pl.loop(0, 4)
    def _(lg_i):
        lanes = pl.ds(pl.multiple_of(lg_i * 128, 128), 128)
        q = jnp.concatenate([qw[0, 0, :, lanes], qw[1, 0, :, lanes]], axis=0)
        k = jnp.concatenate([qw[0, 1, :, lanes], qw[1, 1, :, lanes]], axis=0)
        v = jnp.concatenate([qw[0, 2, :, lanes], qw[1, 2, :, lanes]], axis=0)
        gs = jnp.concatenate([gw[0, :, lanes], gw[1, :, lanes]], axis=0)
        dq = jnp.zeros((TOK, 128), F32)
        dk = jnp.zeros((TOK, 128), F32)
        dv = jnp.zeros((TOK, 128), F32)
        for h in range(4):
            hm = head_mask(h)
            gm = gs * hm
            pr = probs[lg_i * 4 + h]
            wt = pr.astype(BF16)
            pgrad = dot_nt(gm, v)
            delta = jnp.sum(wt.astype(F32) * pgrad, axis=-1, keepdims=True)
            sg = (pr * (pgrad - delta)).astype(BF16)
            dq = dq + dot(sg, k * hm)
            dk = dk + dot_tn(sg, q * hm)
            dv = dv + dot_tn(wt, gm)
        agrad[0, :, lanes] = (dq * inv_sqrt).astype(BF16)
        agrad[1, :, lanes] = (dk * inv_sqrt).astype(BF16)
        agrad[2, :, lanes] = dv.astype(BF16)

    asend[...] = agrad[:, pl.ds(HALF, HALF), :]
    halo_a = remote(asend, arecv, h_ss.at[2], h_rs.at[2], me_e, after)
    halo_a.start()
    for r in range(half_rows):
        for k in range(3):
            attn_out[k, half_rows + r] = agrad[k, pl.ds(r * PADW, WIN), :]

    for m, out in ((0, up_out), (1, down_out)):
        for j in range(2):
            zsent[2 * (2 * m + j) + 1].wait_recv()
            zlast[2 * m + j].wait_recv()
            out[j] = grads[m, j, mz] + zrecv[1, m, j].astype(F32) + zrecv[2, m, j].astype(F32)

    halo_a.wait_recv()
    for r in range(half_rows):
        for k in range(3):
            attn_out[k, r] = arecv[k, pl.ds(r * PADW, WIN), :]

    for cp in (*own_w, *fwd_w, *fwd_x, *sums, *zsent, *zlast, halo_q, halo_g, halo_a):
        cp.wait_send()
    for grp in range(4):
        for which in range(2):
            x_recv(which, grp).wait_send()


def per_device(attn_inputs, residual, logits, expert_ids, keep_mask, cotangent, up_weight, down_weight):
    vmem = pl.BlockSpec(memory_space=pltpu.VMEM)
    dma = pltpu.SemaphoreType.DMA
    outs = pl.pallas_call(
        kernel,
        out_shape=(
            jax.ShapeDtypeStruct((3, WIN, WIN, C), BF16),
            jax.ShapeDtypeStruct((WIN, WIN, C), BF16),
            jax.ShapeDtypeStruct((2, C, HID), F32),
            jax.ShapeDtypeStruct((2, C, HID), F32),
            jax.ShapeDtypeStruct((WIN, WIN, EXPERTS), F32),
        ),
        in_specs=[vmem] * 8,
        out_specs=(vmem,) * 5,
        scratch_shapes=[
            pltpu.VMEM((2, 3, HALF, C), BF16),
            pltpu.VMEM((3, HALF, C), BF16),
            pltpu.VMEM((2, HALF, C), BF16),
            pltpu.VMEM((HALF, C), BF16),
            pltpu.VMEM((3, TOK, C), BF16),
            pltpu.VMEM((3, HALF, C), BF16),
            pltpu.VMEM((3, HALF, C), BF16),
            pltpu.VMEM((TOK, C), BF16),
            pltpu.VMEM((TOK, C), BF16),
            pltpu.VMEM((TOK, EXPERTS), F32),
            pltpu.VMEM((TOK, 2), I32),
            pltpu.VMEM((TOK, 2), I32),
            pltpu.VMEM((TOK, 128), F32),
            pltpu.VMEM((TOK, C), BF16),
            pltpu.VMEM((HEADS, TOK, TOK), F32),
            pltpu.VMEM((TOK, TOK), BF16),
            pltpu.VMEM((TOK, TOK), F32),
            pltpu.VMEM((NE, 48, C), BF16),
            pltpu.VMEM((NE, 48, C), BF16),
            pltpu.VMEM((NX, 4, 2, 2, 48, C), BF16),
            pltpu.VMEM((NZ, 2, 2, C, HID), BF16),
            pltpu.VMEM((2, 2, C, NZ * HID), BF16),
            pltpu.VMEM((NX, 2, 192, NZ * HID), BF16),
            pltpu.VMEM((NX, 2, 192, NZ * HID), BF16),
            pltpu.VMEM((NX, 4, 112, C), F32),
            pltpu.VMEM((12, 112, C), BF16),
            pltpu.VMEM((12, 112, C), BF16),
            pltpu.VMEM((NE, 32, C), BF16),
            pltpu.VMEM((NE, 32, C), BF16),
            pltpu.VMEM((2, 2, NZ, C, HID), F32),
            pltpu.VMEM((3, 2, 2, C, HID), BF16),
            pltpu.VMEM((3, 2, 2, C, HID), BF16),
            dma((NE,)), dma((NE,)),
            dma((3, 4)), dma((3, 4)),
            dma((3, 2)), dma((3, 2)),
            dma((12,)), dma((12,)),
            dma((NE,)), dma((NE,)),
            dma((3, 2, 2)), dma((3, 2, 2)),
            dma((3,)), dma((3,)),
        ],
        compiler_params=pltpu.CompilerParams(
            collective_id=0, has_side_effects=True, vmem_limit_bytes=56 * 1024 * 1024
        ),
    )(
        attn_inputs[:, 0], residual[0], logits[0], expert_ids[0], keep_mask[0], cotangent[0],
        up_weight, down_weight,
    )
    attn_grad, res_grad, up_grad, down_grad, logit_grad = outs
    return attn_grad[:, None], res_grad[None], up_grad, down_grad, logit_grad[None]


def solution(mesh):
    in_specs = (
        P(None, "expert", "space", None, None),
        P("expert", "space", None, None),
        P("expert", "space", None, None),
        P("expert", "space", None, None),
        P("expert", "space", None, None),
        P("expert", "space", None, None),
        P("expert", None, "space"),
        P("expert", None, "space"),
    )
    out_specs = (
        P(None, "expert", "space", None, None),
        P("expert", "space", None, None),
        P("expert", None, "space"),
        P("expert", None, "space"),
        P("expert", "space", None, None),
    )
    return jax.shard_map(
        per_device, mesh=mesh, in_specs=in_specs, out_specs=out_specs, check_vma=False
    )
```

time: 739 us -> 172 us (0.23)
  waiting for transfers between devices: 548 us -> 0 us
  Pallas kernels: 0 us -> 159 us
  starting transfers between devices: 45.5 us -> 0 us
  local copies, waits for them, and re-layouts: 53.7 us -> 9.43 us
  matrix products: 35.3 us -> 0 us
  blocking collectives: 20.8 us -> 0 us
  other arithmetic: 18 us -> 0 us
  between operations: 14.6 us -> 0.66 us
    reduce_scatter x2 -> x0, waiting for transfers between devices: 279 us -> none  [the longest x1 189 us: per_device(): lax.psum_scatter(second_store, 'space', scatter_dimension=2, tiled=True)]
    all_gather x2 -> x0, waiting for transfers between devices: 189 us -> none  [the longest x1 113 us: per_device(): down_piece = lax.all_gather(down_weight, 'space', axis=2, tiled=True)]
    pallas_call x0 -> x1, Pallas kernels: none -> 159 us  [per_device(): pl.pallas_call(kernel, out_shape=(jax.ShapeDtypeStruct((3, WIN, WIN, C),...]
    ppermute x3 -> x0, waiting for transfers between devices: 40.6 us -> none  [from_behind(): return lax.ppermute(block, axis, route)]
    all_to_all x4 -> x0, waiting for transfers between devices: 38.6 us -> none  [the longest x1 14.3 us: per_device(): lax.all_to_all(back_grad, 'expert', split_axis=1, concat_axis=1, tiled=True)]
    dot_general x11 -> x0, matrix products: 32 us -> none  [the longest x1 5.65 us: per_device(): jnp.einsum('erc,ecf->erf', scaled, down_piece, preferred_element_type=jnp...]
    all_to_all x4 -> x0, starting transfers between devices: 30.5 us -> none  [the longest x1 11.5 us: per_device(): lax.all_to_all(send_cot, 'expert', split_axis=1, concat_axis=1, tiled=True)]
    all_to_all x1 -> x0, blocking collectives: 20.8 us -> none  [per_device(): lax.all_to_all(send_scaled, 'expert', split_axis=1, concat_axis=1, tiled=...]
  transfers between devices with their start and end apart: 11 -> 0, of which waited for: 10 -> 0; matrix products, arithmetic and copies ran while one was open for 9% -> 0% of each run, Pallas kernels for 0% -> 0%
where the time goes in v2:
time: 172 us; the launch traced here: 169 us
  Pallas kernels  159 us (92%)
  local copies, waits for them, and re-layouts  9.43 us (5%)
    pallas_call x1, Pallas kernels, per_device(): pl.pallas_call(kernel, out_shape=(jax.ShapeDtypeStruct((3, WIN, WIN, C),...  159 us
    unnamed x18, local copies, waits for them, and re-layouts  9.43 us

profile of v2, /device:TPU:24, one launch (start us, length us, event | category | flops | bytes accessed | tf_op | source)
XLA Modules:
  0.0 169.5 jit_solution(9370265946243961297)
XLA Ops:
  0.6 0.0 copy-start.3
  0.6 1.5 copy.19
  2.2 0.0 copy-done.3
  2.2 0.0 copy-start.4
  2.2 0.8 copy.13
  3.0 0.0 copy-done.4
  3.0 0.8 copy.14
  3.8 159.4 %shard_map.119 = (bf16[3,12,12,512]{3,2,1,0:T(8,128)(2,1)}, bf16[12,12,512]{2,1,0:T(8,128)(2,1)}, f32[2,512,128]{2,1,0:T(8,128)}, f32[2,512,128]{2,1,0:T(8,128)}, f32[12,12,32]{2,1,0:T(8,128)}) custom-call(bf16[3,12,12,512]{3,2,1,0:T(8,128)(2,1)} %bitcast.13, bf16[12,12,512]{2,1,0:T(8,128)(2,1)} %bitcast.18, f32[12,12,32]{2,1,0:T(8,128)} %bitcast.17, ...), custom_call_target="tpu_custom_call" | custom-call | tf_op jit(solution)/shard_map/pallas_call | solution.py:541
  163.2 1.6 copy.16
  164.8 0.0 copy-start.2
  164.8 0.0 copy-start.1
  164.8 2.0 %copy.24 = bf16[3,1,12,12,512]{4,3,2,1,0:T(8,128)(2,1)} copy(bf16[3,1,12,12,512]{4,3,2,1,0:T(8,128)(2,1)} %bitcast.14) | data formatting | bytes 884736
  166.8 0.0 copy-done.2
  166.8 0.7 copy.25
  167.4 0.0 copy-done.1
  167.4 0.0 copy-start
  167.4 0.8 copy.26
  168.2 0.4 copy-done
  168.7 0.8 copy.27
Async XLA Ops:
  0.6 1.5 copy-start.3
  2.2 0.8 copy-start.4
  164.8 2.0 %copy-start.2 = (bf16[12,12,512]{2,1,0:T(8,128)(2,1)S(1)}, bf16[12,12,512]{2,1,0:T(8,128)(2,1)}, u32[]{:S(2)}) copy-start(bf16[12,12,512]{2,1,0:T(8,128)(2,1)} %get-tuple-element.11) | copy-start | bytes 442372
  164.8 2.7 %copy-start.1 = (f32[2,512,128]{2,1,0:T(8,128)S(1)}, f32[2,512,128]{2,1,0:T(8,128)}, u32[]{:S(2)}) copy-start(f32[2,512,128]{2,1,0:T(8,128)} %get-tuple-element.27) | copy-start | bytes 1572868
  167.4 1.2 copy-start

commit v3 on v2

--- a/solution.py
+++ b/solution.py
@@ -16,6 +16,8 @@
 NE = 16
 NX = 4
 NZ = 4
+RING = 8
+NYC = 8
 HID = 128
 NORM_EPS = 1e-06
 SCORE_MASK = -100.0
@@ -77,13 +79,14 @@
     x1 = mx + 1 - 2 * (mx % 2)
     x3 = NX - 1 - mx
     x2 = NX - 1 - x1
-    z1 = mz + 1 - 2 * (mz % 2)
-    z3 = NZ - 1 - mz
-    z2 = NZ - 1 - z1
+    me_yc = me_e % NYC
+    zr = zhi * NZ + mz
     dev_x1 = x1 * NZ + mz
     dev_x3 = x3 * NZ + mz
-    dev_z1 = mx * NZ + z1
-    dev_z2 = mx * NZ + z2
+    ring = []
+    for step in (1, RING - 1):
+        to = (zr + step) % RING
+        ring.append(((to // NZ) * NYC + me_yc, mx * NZ + to % NZ))
     after = (me_s + 1) % (NX * NZ)
     before = (me_s + NX * NZ - 1) % (NX * NZ)
 
@@ -100,11 +103,13 @@
             barrier, inc=1, device_id={"expert": e, "space": s}, device_id_type=pl.DeviceIdType.MESH
         )
 
-    @pl.loop(1, NE)
+    @pl.loop(1, NYC)
     def _(i):
-        greet((me_e + i) % NE, me_s)
-
-    for s in (dev_x1, dev_x3, dev_z1, dev_z2, after, before):
+        greet(zhi * NYC + (me_yc + i) % NYC, me_s)
+
+    for e, s in ring:
+        greet(e, s)
+    for s in (dev_x1, dev_x3, after, before):
         greet(me_e, s)
 
     half_rows = WIN // 2
@@ -127,13 +132,40 @@
             qsend[k, pl.ds(r * PADW, WIN), :] = attn_ref[k, r]
             qw[0, k, pl.ds(r * PADW, WIN), :] = attn_ref[k, half_rows + r]
 
-    pl.semaphore_wait(barrier, NE - 1 + 6)
-
-    own_w = []
-    for m, ref in ((0, up_ref), (1, down_ref)):
-        own_w.append(remote(ref, w_all.at[mz, m], w_ss.at[0, m], w_rs.at[0, m], me_e, dev_z2))
-    for m, ref in ((0, up_ref), (1, down_ref)):
-        own_w.append(remote(ref, w_all.at[mz, m], w_ss.at[1, m], w_rs.at[1, m], me_e, dev_z1))
+    pl.semaphore_wait(barrier, NYC - 1 + 6)
+
+    def weight_copy(way, step, m, j):
+        chunk = (zr - step) % RING if way == 0 else (zr + step) % RING
+        src = (up_ref, down_ref)[m].at[j] if step == 0 else w_all.at[chunk, m, j]
+        return remote(
+            src, w_all.at[chunk, m, j], w_ss.at[way, step, m, j], w_rs.at[way, step, m, j], *ring[way]
+        )
+
+    def weight_arrived(way, step, m, j):
+        chunk = (zr - 1 - step) % RING if way == 0 else (zr + 1 + step) % RING
+        remote(
+            w_all.at[chunk, m, j], w_all.at[chunk, m, j], w_ss.at[way, step, m, j],
+            w_rs.at[way, step, m, j], *ring[way],
+        ).wait_recv()
+
+    pieces = [(m, j) for m in range(2) for j in range(2)]
+    sent_w = []
+
+    def start_weight(way, step, m, j):
+        cp = weight_copy(way, step, m, j)
+        cp.start()
+        sent_w.append(cp)
+
+    def forward_weights(step):
+        for m, j in pieces:
+            for way in range(2):
+                weight_arrived(way, step - 1, m, j)
+                if step < 3 or m == way:
+                    start_weight(way, step, m, j)
+
+    for m, j in pieces:
+        for way in range(2):
+            start_weight(way, 0, m, j)
     halo_q = remote(qsend, qw.at[1], h_ss.at[0], h_rs.at[0], me_e, before)
 
     resid = resid_s[...].astype(F32)
@@ -175,31 +207,29 @@
     rem = row - 48 * src4
     second = ge(rem, 24)
 
-    @pl.loop(0, 4)
-    def _(k):
-        ch = (2 * (1 - zhi) + k) % 4
-        q = (ch * 4 + src4) * 24 + rem - 24 * second
-        m1 = q == q1_row
-        m2 = q == q2_row
-        is_norm = second == 0
-        pn = ones_where((m1 | m2) & is_norm)
-        ps1 = ones_where(m1 & (second == 1))
-        ps2 = ones_where(m2 & (second == 1))
-        built = dot(pn, normed) + dot(ps1, scaled1) + dot(ps2, scaled2)
-        send_rows[pl.ds(ch * 4, 4)] = built.astype(BF16).reshape(4, 48, C)
+    @pl.loop(0, 2)
+    def _(h):
+        for p in range(2):
+            q = (p * NYC + h * 4 + src4) * 24 + rem - 24 * second
+            m1 = q == q1_row
+            m2 = q == q2_row
+            pn = ones_where((m1 | m2) & (second == 0))
+            ps1 = ones_where(m1 & (second == 1))
+            ps2 = ones_where(m2 & (second == 1))
+            built = dot(pn, normed) + dot(ps1, scaled1) + dot(ps2, scaled2)
+            send_rows[pl.ds(h * 4, 4), p] = built.astype(BF16).reshape(4, 48, C)
         for s in range(4):
-            to = ch * 4 + s
-
-            @pl.when(to != me_e)
+            to = h * 4 + s
+
+            @pl.when(to != me_yc)
             def _():
                 remote(
-                    send_rows.at[to], recv_rows.at[me_e], d_ss.at[to], d_rs.at[me_e], to, me_s
+                    send_rows.at[to], recv_rows.at[me_yc], d_ss.at[to], d_rs.at[me_yc],
+                    zhi * NYC + to, me_s,
                 ).start()
 
-    for cp in own_w:
-        cp.start()
     halo_q.start()
-    recv_rows[me_e] = send_rows[me_e]
+    recv_rows[me_yc] = send_rows[me_yc]
 
     b96 = ge(row, 96)
     o2 = row - 96 * b96
@@ -234,35 +264,31 @@
             ex = jnp.exp(sc - jnp.max(sc, axis=-1, keepdims=True))
             probs[lg_i * 4 + h] = ex / jnp.sum(ex, axis=-1, keepdims=True)
 
-    @pl.loop(0, 4)
-    def _(k):
-        grp = (2 * zhi + k) % 4
+    @pl.loop(0, 2)
+    def _(g):
         for s in range(4):
-            frm = grp * 4 + s
-
-            @pl.when(frm != me_e)
+            frm = g * 4 + s
+
+            @pl.when(frm != me_yc)
             def _():
                 remote(
-                    send_rows.at[frm], recv_rows.at[frm], d_ss.at[frm], d_rs.at[frm], frm, me_s
+                    send_rows.at[frm], recv_rows.at[frm], d_ss.at[frm], d_rs.at[frm],
+                    zhi * NYC + frm, me_s,
                 ).wait()
 
-        block = recv_rows[pl.ds(grp * 4, 4)].reshape(TOK, C)
-        rows_all[mx, grp] = dot(perm_s[...], block).astype(BF16).reshape(2, 2, 48, C)
-        remote(
-            rows_all.at[mx, grp], rows_all.at[mx, grp], g_ss.at[0, grp], g_rs.at[0, grp], me_e, dev_x1
-        ).start()
-        remote(
-            rows_all.at[mx, grp], rows_all.at[mx, grp], g_ss.at[1, grp], g_rs.at[1, grp], me_e, dev_x3
-        ).start()
-
-    fwd_w = []
-    for m in range(2):
-        own_w[m].wait_recv()
-        cp = remote(
-            w_all.at[z2, m], w_all.at[z2, m], w_ss.at[2, m], w_rs.at[2, m], me_e, dev_z1
-        )
-        cp.start()
-        fwd_w.append(cp)
+        for p in range(2):
+            grp = 2 * p + g
+            block = recv_rows[pl.ds(g * 4, 4), p].reshape(TOK, C)
+            rows_all[mx, grp] = dot(perm_s[...], block).astype(BF16).reshape(2, 2, 48, C)
+            for which, dev in ((0, dev_x1), (1, dev_x3)):
+                remote(
+                    rows_all.at[mx, grp], rows_all.at[mx, grp], g_ss.at[which, grp],
+                    g_rs.at[which, grp], me_e, dev,
+                ).start()
+
+    forward_weights(1)
+    w_all[zr, 0] = up_ref[...]
+    w_all[zr, 1] = down_ref[...]
 
     def x_recv(which, grp):
         frm, dev = ((x1, dev_x1), (x3, dev_x3))[which]
@@ -272,7 +298,8 @@
         )
 
     fwd_x = []
-    for grp in range(4):
+
+    def forward_rows(grp):
         which = 0 if grp < 2 else 1
         x_recv(which, grp).wait_recv()
         frm, dev = ((x1, dev_x3), (x3, dev_x1))[which]
@@ -282,19 +309,28 @@
         cp.start()
         fwd_x.append(cp)
 
-    for m in range(2):
-        own_w[2 + m].wait_recv()
-        fwd_w[m].wait_recv()
-    w_all[mz, 0] = up_ref[...]
-    w_all[mz, 1] = down_ref[...]
-    for m in range(2):
+    forward_rows(0)
+    forward_rows(2)
+    forward_weights(2)
+    forward_rows(1)
+    forward_rows(3)
+    forward_weights(3)
+    for way in range(2):
         for j in range(2):
-            wcat[m, j] = jnp.concatenate([w_all[c, m, j] for c in range(NZ)], axis=1)
-
-    def expert_rows(b):
+            weight_arrived(way, 3, way, j)
+    for grp in (2, 3):
+        x_recv(0, grp).wait_recv()
+    for grp in (0, 1):
+        x_recv(1, grp).wait_recv()
+    for cp in fwd_x:
+        cp.wait_recv()
+
+    def expert_rows(p):
+        for m, j in pieces:
+            wcat[m, j] = jnp.concatenate([w_all[p * NZ + c, m, j] for c in range(NZ)], axis=1)
         for j in range(2):
-            xn = rows_all[b, :, 0, j].reshape(192, C)
-            xsc = rows_all[b, :, 1, j].reshape(192, C)
+            xn = rows_all[:, pl.ds(2 * p, 2), 0, j].reshape(384, C)
+            xsc = rows_all[:, pl.ds(2 * p, 2), 1, j].reshape(384, C)
             pre = dot(xn, wcat[0, j])
             sq = pre * pre
             t = jnp.tanh(GELU_C * pre * (1.0 + GELU_A * sq))
@@ -303,97 +339,81 @@
             dact = dot(xsc, wcat[1, j])
             dsum = jnp.sum(act.astype(F32) * dact, axis=-1, keepdims=True)
             pg = (dact * slope).astype(BF16)
-            act_s[b, j] = act
-            pg_s[b, j] = pg
+            act_s[j] = act
+            pg_s[j] = pg
             rg = dot_nt(pg, wcat[0, j])
-            part[b, :, pl.ds(j * 48, 48), :] = rg.reshape(4, 48, C)
+            part[:, pl.ds(2 * p, 2), pl.ds(j * 48, 48), :] = rg.reshape(4, 2, 48, C)
             hit = iota((48, C), 1) == iota((48, C), 0) + j * 48
-            for g in range(4):
-                line = jnp.sum(
-                    jnp.where(hit, dsum[g * 48 : (g + 1) * 48], 0.0), axis=0, keepdims=True
-                )
-                if j == 0:
+            for b in range(NX):
+                for g in range(2):
+                    lo = (2 * b + g) * 48
+                    line = jnp.sum(jnp.where(hit, dsum[lo : lo + 48], 0.0), axis=0, keepdims=True)
                     tail = jnp.where(iota((16, C), 0) == 0, line, 0.0)
-                    part[b, g, pl.ds(96, 16), :] = tail
-                else:
-                    tail = jnp.where(iota((16, C), 0) == 0, line, 0.0)
-                    part[b, g, pl.ds(96, 16), :] += tail
+                    if j == 0:
+                        part[b, 2 * p + g, pl.ds(96, 16), :] = tail
+                    else:
+                        part[b, 2 * p + g, pl.ds(96, 16), :] += tail
+
+    def expert_grads(p):
+        for m, j in pieces:
+            left = rows_all[:, pl.ds(2 * p, 2), m, j].reshape(384, C)
+            full = dot_tn(left, (pg_s, act_s)[m][j])
+            for c in range(NZ):
+                grads[p * NZ + c, m, j] = full[:, c * HID : (c + 1) * HID]
 
     def x_send(n, dev, slot, sem):
         return remote(xs.at[n], xr.at[slot], x_ss.at[n], x_rs.at[sem], me_e, dev)
 
-    expert_rows(mx)
-    x_recv(0, 2).wait_recv()
-    x_recv(0, 3).wait_recv()
-    expert_rows(x1)
-    sums = []
-    for g in (0, 1):
-        xs[g] = split_tail(part[x1, g])
-        sums.append(x_send(g, dev_x1, g, g))
-        sums[-1].start()
-    x_recv(1, 0).wait_recv()
-    x_recv(1, 1).wait_recv()
-    expert_rows(x3)
-    for g in (2, 3):
-        xs[4 + g] = split_tail(part[x3, g])
-        sums.append(x_send(4 + g, dev_x3, 4 + g, 4 + g))
-        sums[-1].start()
-    for cp in fwd_x:
-        cp.wait_recv()
-    expert_rows(x2)
-    for g in (0, 1):
-        xs[8 + g] = split_tail(part[x2, g])
-        sums.append(x_send(8 + g, dev_x1, 8 + g, 8 + g))
-        sums[-1].start()
-    for g in (2, 3):
-        xs[8 + g] = split_tail(part[x2, g])
-        sums.append(x_send(8 + g, dev_x3, 8 + g, 8 + g))
-        sums[-1].start()
+    sent_z = []
+
+    def start_sum(way, step, m, j, add):
+        to = (zr + 4 - step) % RING if way == 0 else (zr + 4 + step) % RING
+        value = grads[to, m, j]
+        if add:
+            cp = remote(
+                zsend.at[way, step - 1, m, j], zrecv.at[way, step - 1, m, j],
+                z_ss.at[way, step - 1, m, j], z_rs.at[way, step - 1, m, j], *ring[way],
+            )
+            cp.wait_recv()
+            value = value + zrecv[way, step - 1, m, j].astype(F32)
+        zsend[way, step, m, j] = value.astype(BF16)
+        cp = remote(
+            zsend.at[way, step, m, j], zrecv.at[way, step, m, j], z_ss.at[way, step, m, j],
+            z_rs.at[way, step, m, j], *ring[way],
+        )
+        cp.start()
+        sent_z.append(cp)
 
     def x_got(slot):
         return remote(xs.at[slot], xr.at[slot], x_ss.at[slot], x_rs.at[slot], me_e, dev_x1)
 
-    zsent = []
-
-    def weight_grad(m, j):
-        left = rows_all[:, :, m, j].reshape(4 * 192, C)
-        right = (pg_s, act_s)[m][:, j].reshape(4 * 192, C)
-        full = dot_tn(left, right)
-        for c in range(NZ):
-            grads[m, j, c] = full[:, c * HID : (c + 1) * HID]
-        zsend[0, m, j] = grads[m, j, z3].astype(BF16)
-        zsend[1, m, j] = grads[m, j, z1].astype(BF16)
-        for n in range(2):
-            cp = remote(
-                zsend.at[n, m, j], zrecv.at[n, m, j], z_ss.at[n, m, j], z_rs.at[n, m, j], me_e, dev_z1
-            )
-            cp.start()
-            zsent.append(cp)
-
-    def z_forward(m, j):
-        zsent[2 * (2 * m + j)].wait_recv()
-        zsend[2, m, j] = (grads[m, j, z2] + zrecv[0, m, j].astype(F32)).astype(BF16)
-        cp = remote(
-            zsend.at[2, m, j], zrecv.at[2, m, j], z_ss.at[2, m, j], z_rs.at[2, m, j], me_e, dev_z2
-        )
-        cp.start()
-        zlast.append(cp)
-
-    zlast = []
-    weight_grad(0, 0)
-    weight_grad(0, 1)
+    sums = []
+    def send_sum(slot, dev, value):
+        xs[slot] = split_tail(value)
+        sums.append(x_send(slot, dev, slot, slot))
+        sums[-1].start()
+
+    expert_rows(1 - zhi)
+    expert_grads(1 - zhi)
+    for m, j in pieces:
+        start_sum(m, 0, m, j, False)
+    expert_rows(zhi)
+    for g in (0, 1):
+        send_sum(8 + g, dev_x1, part[x2, g])
+        send_sum(10 + g, dev_x3, part[x2, 2 + g])
+    for g in (0, 1):
+        send_sum(g, dev_x1, part[x1, g])
+        send_sum(6 + g, dev_x3, part[x3, 2 + g])
+    expert_grads(zhi)
+    for m, j in pieces:
+        start_sum(1 - m, 1, m, j, False)
+    for m, j in pieces:
+        start_sum(m, 1, m, j, True)
     for g in (0, 1):
         x_got(8 + g).wait_recv()
-        xs[4 + g] = split_tail(part[x3, g] + xr[8 + g].astype(F32))
-        sums.append(x_send(4 + g, dev_x3, 4 + g, 4 + g))
-        sums[-1].start()
-    for g in (2, 3):
-        x_got(8 + g).wait_recv()
-        xs[g] = split_tail(part[x1, g] + xr[8 + g].astype(F32))
-        sums.append(x_send(g, dev_x1, g, g))
-        sums[-1].start()
-    weight_grad(1, 0)
-    weight_grad(1, 1)
+        send_sum(4 + g, dev_x3, part[x3, g] + xr[8 + g].astype(F32))
+        x_got(10 + g).wait_recv()
+        send_sum(2 + g, dev_x1, part[x1, 2 + g] + xr[10 + g].astype(F32))
 
     ro = iota((128, 112), 0)
     rs = ge(ro, 32) + ge(ro, 64) + ge(ro, 96)
@@ -401,31 +421,35 @@
     rj = ge(rq, 12)
     want = jnp.where(rq < 24, rj * 48 + rs * 12 + rq - 12 * rj, jnp.where(rq < 26, rq + 72, -1))
     back = ones_where(iota((128, 112), 1) == want)
-    for g in range(4):
-        x_got(g).wait_recv()
-        x_got(4 + g).wait_recv()
-        total = split_tail(part[mx, g] + xr[g].astype(F32) + xr[4 + g].astype(F32))
-        ret_send[pl.ds(g * 4, 4)] = dot(back, total).astype(BF16).reshape(4, 32, C)
+    for g in range(2):
+        for p in range(2):
+            grp = 2 * p + g
+            x_got(grp).wait_recv()
+            x_got(4 + grp).wait_recv()
+            total = split_tail(part[mx, grp] + xr[grp].astype(F32) + xr[4 + grp].astype(F32))
+            ret_send[pl.ds(g * 4, 4), p] = dot(back, total).astype(BF16).reshape(4, 32, C)
         for s in range(4):
             to = g * 4 + s
 
-            @pl.when(to != me_e)
+            @pl.when(to != me_yc)
             def _():
                 remote(
-                    ret_send.at[to], ret_recv.at[me_e], r_ss.at[to], r_rs.at[me_e], to, me_s
+                    ret_send.at[to], ret_recv.at[me_yc], r_ss.at[to], r_rs.at[me_yc],
+                    zhi * NYC + to, me_s,
                 ).start()
 
-    ret_recv[me_e] = ret_send[me_e]
-    for m in range(2):
-        for j in range(2):
-            z_forward(m, j)
-
-    @pl.loop(0, NE)
+    ret_recv[me_yc] = ret_send[me_yc]
+    for m, j in pieces:
+        for way in range(2):
+            start_sum(way, 2, m, j, True)
+
+    @pl.loop(0, NYC)
     def _(frm):
-        @pl.when(frm != me_e)
+        @pl.when(frm != me_yc)
         def _():
             remote(
-                ret_send.at[frm], ret_recv.at[frm], r_ss.at[frm], r_rs.at[frm], frm, me_s
+                ret_send.at[frm], ret_recv.at[frm], r_ss.at[frm], r_rs.at[frm],
+                zhi * NYC + frm, me_s,
             ).wait()
 
     returned = ret_recv[...].reshape(NE * 32, C)
@@ -440,8 +464,9 @@
     q1 = id1 * CAP + slot1
     q2 = id2 * CAP + slot2
     col = iota((TOK, NE * 32), 1)
-    dev = lax.shift_right_arithmetic(col, 5)
-    pos = col - 32 * dev
+    block_of = lax.shift_right_arithmetic(col, 5)
+    pos = col - 32 * block_of
+    dev = lax.shift_right_arithmetic(block_of, 1) + NYC * (block_of % 2)
     at = dev * 24 + pos
     pick = ones_where(((at == q1) | (at == q2)) & (pos < 24))
     norm_grad = dot(pick, returned)
@@ -482,6 +507,10 @@
     lg_s[...] = (oh1 - oh2) * part1 + EXPERTS * rp * (share - share_mean)
     for r in range(WIN):
         logit_out[r] = lg_s[pl.ds(r * PADW, WIN), :]
+
+    for m, j in pieces:
+        for way in range(2):
+            start_sum(way, 3, m, j, True)
 
     halo_g.wait_recv()
 
@@ -519,16 +548,21 @@
 
     for m, out in ((0, up_out), (1, down_out)):
         for j in range(2):
-            zsent[2 * (2 * m + j) + 1].wait_recv()
-            zlast[2 * m + j].wait_recv()
-            out[j] = grads[m, j, mz] + zrecv[1, m, j].astype(F32) + zrecv[2, m, j].astype(F32)
+            value = grads[zr, m, j]
+            for way in range(2):
+                remote(
+                    zsend.at[way, 3, m, j], zrecv.at[way, 3, m, j], z_ss.at[way, 3, m, j],
+                    z_rs.at[way, 3, m, j], *ring[way],
+                ).wait_recv()
+                value = value + zrecv[way, 3, m, j].astype(F32)
+            out[j] = value
 
     halo_a.wait_recv()
     for r in range(half_rows):
         for k in range(3):
             attn_out[k, r] = arecv[k, pl.ds(r * PADW, WIN), :]
 
-    for cp in (*own_w, *fwd_w, *fwd_x, *sums, *zsent, *zlast, halo_q, halo_g, halo_a):
+    for cp in (*sent_w, *fwd_x, *sums, *sent_z, halo_q, halo_g, halo_a):
         cp.wait_send()
     for grp in range(4):
         for which in range(2):
@@ -567,27 +601,27 @@
             pltpu.VMEM((HEADS, TOK, TOK), F32),
             pltpu.VMEM((TOK, TOK), BF16),
             pltpu.VMEM((TOK, TOK), F32),
-            pltpu.VMEM((NE, 48, C), BF16),
-            pltpu.VMEM((NE, 48, C), BF16),
+            pltpu.VMEM((NYC, 2, 48, C), BF16),
+            pltpu.VMEM((NYC, 2, 48, C), BF16),
             pltpu.VMEM((NX, 4, 2, 2, 48, C), BF16),
-            pltpu.VMEM((NZ, 2, 2, C, HID), BF16),
+            pltpu.VMEM((RING, 2, 2, C, HID), BF16),
             pltpu.VMEM((2, 2, C, NZ * HID), BF16),
-            pltpu.VMEM((NX, 2, 192, NZ * HID), BF16),
-            pltpu.VMEM((NX, 2, 192, NZ * HID), BF16),
+            pltpu.VMEM((2, 384, NZ * HID), BF16),
+            pltpu.VMEM((2, 384, NZ * HID), BF16),
             pltpu.VMEM((NX, 4, 112, C), F32),
             pltpu.VMEM((12, 112, C), BF16),
             pltpu.VMEM((12, 112, C), BF16),
-            pltpu.VMEM((NE, 32, C), BF16),
-            pltpu.VMEM((NE, 32, C), BF16),
-            pltpu.VMEM((2, 2, NZ, C, HID), F32),
-            pltpu.VMEM((3, 2, 2, C, HID), BF16),
-            pltpu.VMEM((3, 2, 2, C, HID), BF16),
-            dma((NE,)), dma((NE,)),
+            pltpu.VMEM((NYC, 2, 32, C), BF16),
+            pltpu.VMEM((NYC, 2, 32, C), BF16),
+            pltpu.VMEM((RING, 2, 2, C, HID), F32),
+            pltpu.VMEM((2, 4, 2, 2, C, HID), BF16),
+            pltpu.VMEM((2, 4, 2, 2, C, HID), BF16),
+            dma((NYC,)), dma((NYC,)),
             dma((3, 4)), dma((3, 4)),
-            dma((3, 2)), dma((3, 2)),
+            dma((2, 4, 2, 2)), dma((2, 4, 2, 2)),
             dma((12,)), dma((12,)),
-            dma((NE,)), dma((NE,)),
-            dma((3, 2, 2)), dma((3, 2, 2)),
+            dma((NYC,)), dma((NYC,)),
+            dma((2, 4, 2, 2)), dma((2, 4, 2, 2)),
             dma((3,)), dma((3,)),
         ],
         compiler_params=pltpu.CompilerParams(

time: 172 us -> 130 us (0.76)
  Pallas kernels: 159 us -> 118 us
    pallas_call x1, Pallas kernels: 159 us -> 118 us  [per_device(): pl.pallas_call(kernel, out_shape=(jax.ShapeDtypeStruct((3, WIN, WIN, C),...]
where the time goes in v3:
time: 130 us; the launch traced here: 128 us
  Pallas kernels  118 us (91%)
  local copies, waits for them, and re-layouts  9.43 us (7%)
    pallas_call x1, Pallas kernels, per_device(): pl.pallas_call(kernel, out_shape=(jax.ShapeDtypeStruct((3, WIN, WIN, C),...  118 us
    unnamed x18, local copies, waits for them, and re-layouts  9.43 us

profile of v3, /device:TPU:24, one launch (start us, length us, event | category | flops | bytes accessed | tf_op | source)
XLA Modules:
  0.0 128.0 jit_solution(943907069942946321)
XLA Ops:
  0.6 0.0 copy-start.3
  0.6 1.5 %copy.19 = f32[1,12,12,32]{3,2,0,1:T(8,128)} copy(f32[1,12,12,32]{3,0,2,1:T(1,128)} %param.10) | data formatting | bytes 36864
  2.2 0.0 copy-done.3
  2.2 0.0 copy-start.4
  2.2 0.8 copy.13
  3.0 0.0 copy-done.4
  3.0 0.8 copy.14
  3.8 117.9 %shard_map.119 = (bf16[3,12,12,512]{3,2,1,0:T(8,128)(2,1)}, bf16[12,12,512]{2,1,0:T(8,128)(2,1)}, f32[2,512,128]{2,1,0:T(8,128)}, f32[2,512,128]{2,1,0:T(8,128)}, f32[12,12,32]{2,1,0:T(8,128)}) custom-call(bf16[3,12,12,512]{3,2,1,0:T(8,128)(2,1)} %bitcast.13, bf16[12,12,512]{2,1,0:T(8,128)(2,1)} %bitcast.18, f32[12,12,32]{2,1,0:T(8,128)} %bitcast.17, ...), custom_call_target="tpu_custom_call" | custom-call | tf_op jit(solution)/shard_map/pallas_call | solution.py:575
  121.7 1.6 %copy.16 = f32[1,12,12,32]{3,0,2,1:T(1,128)} copy(f32[1,12,12,32]{3,2,1,0:T(8,128)} %bitcast.21) | data formatting | bytes 36864
  123.3 0.0 copy-start.2
  123.3 0.0 copy-start.1
  123.3 2.0 %copy.24 = bf16[3,1,12,12,512]{4,3,2,1,0:T(8,128)(2,1)} copy(bf16[3,1,12,12,512]{4,3,2,1,0:T(8,128)(2,1)} %bitcast.14) | data formatting | bytes 884736
  125.3 0.0 copy-done.2
  125.3 0.7 copy.25
  126.0 0.0 copy-done.1
  126.0 0.0 copy-start
  126.0 0.8 copy.26
  126.8 0.4 copy-done
  127.2 0.8 copy.27
Async XLA Ops:
  0.6 1.5 %copy-start.3 = (s32[1,12,12,2]{2,3,1,0:T(2,128)S(1)}, s32[1,12,12,2]{2,3,1,0:T(2,128)}, u32[]{:S(2)}) copy-start(s32[1,12,12,2]{2,3,1,0:T(2,128)} %param.11) | copy-start | bytes 3460
  2.2 0.8 copy-start.4
  123.3 2.0 %copy-start.2 = (bf16[12,12,512]{2,1,0:T(8,128)(2,1)S(1)}, bf16[12,12,512]{2,1,0:T(8,128)(2,1)}, u32[]{:S(2)}) copy-start(bf16[12,12,512]{2,1,0:T(8,128)(2,1)} %get-tuple-element.11) | copy-start | bytes 442372
  123.3 2.7 %copy-start.1 = (f32[2,512,128]{2,1,0:T(8,128)S(1)}, f32[2,512,128]{2,1,0:T(8,128)}, u32[]{:S(2)}) copy-start(f32[2,512,128]{2,1,0:T(8,128)} %get-tuple-element.27) | copy-start | bytes 1572868
  126.0 1.2 copy-start

commit v4 on v3

--- a/solution.py
+++ b/solution.py
@@ -54,22 +54,22 @@
 
 
 def split_tail(x):
-    total = x[96:97] + x[97:98]
+    total = x[48:49] + x[49:50]
     high = total.astype(BF16).astype(F32)
     low = total - high
     row = iota((16, C), 0)
     tail = jnp.where(row == 0, high, jnp.where(row == 1, low, 0.0))
-    return jnp.concatenate([x[:96], tail], axis=0).astype(BF16)
+    return jnp.concatenate([x[:48], tail], axis=0).astype(BF16)
 
 
 def kernel(
     attn_ref, resid_ref, logit_ref, ids_ref, keep_ref, cot_ref, up_ref, down_ref,
     attn_out, res_out, up_out, down_out, logit_out,
-    qw, qsend, gw, gsend, agrad, asend, arecv,
+    qw, qsend, qrecv, pack_s, gw, gsend, grecv, agrad, asend, arecv,
     resid_s, cot_s, lg_s, ids_s, keep_s, cols, stage, probs, perm_s, bias_s,
-    send_rows, recv_rows, rows_all, w_all, wcat, pg_s, act_s, part, xs, xr,
+    gswap, send_rows, recv_rows, rows_two, rows_all, w_all, pg_s, dots_s, part, xs, xr,
     ret_send, ret_recv, grads, zsend, zrecv,
-    d_ss, d_rs, g_ss, g_rs, w_ss, w_rs, x_ss, x_rs, r_ss, r_rs, z_ss, z_rs, h_ss, h_rs,
+    d_ss, d_rs, g_ss, g_rs, w_ss, w_rs, x_ss, x_rs, r_ss, r_rs, z_ss, z_rs, h_ss, h_rs, s_ss, s_rs,
 ):
     me_e = lax.axis_index("expert")
     me_s = lax.axis_index("space")
@@ -80,6 +80,8 @@
     x3 = NX - 1 - mx
     x2 = NX - 1 - x1
     me_yc = me_e % NYC
+    mine = mx * (NX - 1 - mx) // 2
+    other = 1 - mine
     zr = zhi * NZ + mz
     dev_x1 = x1 * NZ + mz
     dev_x3 = x3 * NZ + mz
@@ -113,8 +115,7 @@
         greet(me_e, s)
 
     half_rows = WIN // 2
-    qw[0] = jnp.zeros((3, HALF, C), BF16)
-    qsend[...] = jnp.zeros((3, HALF, C), BF16)
+    qw[...] = jnp.zeros((2, 3, HALF, C), BF16)
     resid_s[...] = jnp.zeros((TOK, C), BF16)
     cot_s[...] = jnp.zeros((TOK, C), BF16)
     lg_s[...] = jnp.zeros((TOK, EXPERTS), F32)
@@ -129,14 +130,14 @@
         keep_s[at, :] = keep_ref[r]
     for r in range(half_rows):
         for k in range(3):
-            qsend[k, pl.ds(r * PADW, WIN), :] = attn_ref[k, r]
+            qw[1, k, pl.ds(r * PADW, WIN), :] = attn_ref[k, r]
             qw[0, k, pl.ds(r * PADW, WIN), :] = attn_ref[k, half_rows + r]
 
     pl.semaphore_wait(barrier, NYC - 1 + 6)
 
     def weight_copy(way, step, m, j):
         chunk = (zr - step) % RING if way == 0 else (zr + step) % RING
-        src = (up_ref, down_ref)[m].at[j] if step == 0 else w_all.at[chunk, m, j]
+        src = (up_ref, down_ref)[m].at[mine] if step == 0 and j == 0 else w_all.at[chunk, m, j]
         return remote(
             src, w_all.at[chunk, m, j], w_ss.at[way, step, m, j], w_rs.at[way, step, m, j], *ring[way]
         )
@@ -148,7 +149,7 @@
             w_rs.at[way, step, m, j], *ring[way],
         ).wait_recv()
 
-    pieces = [(m, j) for m in range(2) for j in range(2)]
+    pieces = [(m, j) for j in range(2) for m in range(2)]
     sent_w = []
 
     def start_weight(way, step, m, j):
@@ -163,10 +164,26 @@
                 if step < 3 or m == way:
                     start_weight(way, step, m, j)
 
-    for m, j in pieces:
+    swap_w = [
+        remote((up_ref, down_ref)[m].at[other], w_all.at[zr, m, 1], s_ss.at[m], s_rs.at[m], me_e, dev_x1)
+        for m in range(2)
+    ]
+    for m in range(2):
+        swap_w[m].start()
         for way in range(2):
-            start_weight(way, 0, m, j)
-    halo_q = remote(qsend, qw.at[1], h_ss.at[0], h_rs.at[0], me_e, before)
+            start_weight(way, 0, m, 0)
+
+    def packing(count, dense):
+        wide, narrow = count * HALF, dense
+        i = iota((narrow, wide), 0)
+        o = iota((narrow, wide), 1)
+        keep_row = (o % PADW < WIN) & ((o // PADW) * WIN + o % PADW == i)
+        return ones_where(keep_row)
+
+    pack_s[...] = packing(3, 224)
+    qsend[...] = dot(pack_s[...], qw[1].reshape(3 * HALF, C)).astype(BF16)
+    halo_q = remote(qsend, qrecv, h_ss.at[0], h_rs.at[0], me_e, before)
+    halo_q.start()
 
     resid = resid_s[...].astype(F32)
     rms = jnp.sqrt(jnp.mean(resid * resid, axis=-1, keepdims=True) + NORM_EPS)
@@ -202,6 +219,11 @@
         column = jnp.where(lane == i, v, column)
     cols[...] = column
 
+    for m in range(2):
+        swap_w[m].wait_recv()
+        for way in range(2):
+            start_weight(way, 0, m, 1)
+
     row = iota((TOK, 1), 0)
     src4 = ge(row, 48) + ge(row, 96) + ge(row, 144)
     rem = row - 48 * src4
@@ -228,7 +250,6 @@
                     zhi * NYC + to, me_s,
                 ).start()
 
-    halo_q.start()
     recv_rows[me_yc] = send_rows[me_yc]
 
     b96 = ge(row, 96)
@@ -236,7 +257,34 @@
     b48 = ge(o2, 48)
     o3 = o2 - 48 * b48
     s12 = ge(o3, 12) + ge(o3, 24) + ge(o3, 36)
-    perm_s[...] = ones_where(square_c == s12 * 48 + b96 * 24 + b48 * 12 + (o3 - 12 * s12))
+    perm_s[...] = ones_where(square_c == s12 * 48 + b48 * 24 + b96 * 12 + (o3 - 12 * s12))
+
+    @pl.loop(0, 2)
+    def _(g):
+        for s in range(4):
+            frm = g * 4 + s
+
+            @pl.when(frm != me_yc)
+            def _():
+                remote(
+                    send_rows.at[frm], recv_rows.at[frm], d_ss.at[frm], d_rs.at[frm],
+                    zhi * NYC + frm, me_s,
+                ).wait()
+
+        for p in range(2):
+            grp = 2 * p + g
+            block = recv_rows[pl.ds(g * 4, 4), p].reshape(TOK, C)
+            rows_two[grp] = dot(perm_s[...], block).astype(BF16).reshape(2, 2, 48, C)
+            for which, j, dev in ((0, other, dev_x1), (1, mine, dev_x3)):
+                remote(
+                    rows_two.at[grp, j], rows_all.at[mx, grp], g_ss.at[which, grp],
+                    g_rs.at[which, grp], me_e, dev,
+                ).start()
+            rows_all[mx, grp] = rows_two[grp, mine]
+
+    forward_weights(1)
+    w_all[zr, 0, 0] = up_ref[mine]
+    w_all[zr, 1, 0] = down_ref[mine]
 
     pos_r = square_r % PADW
     pos_c = square_c % PADW
@@ -248,6 +296,7 @@
     bias_s[...] = jnp.where(pos_c >= WIN, NO_KEY, bias)
     inv_sqrt = (C // HEADS) ** (-0.5)
     halo_q.wait_recv()
+    qw[1] = dot_tn(pack_s[...], qrecv[...]).astype(BF16).reshape(3, HALF, C)
 
     head_lane = iota((1, 128), 1)
 
@@ -264,32 +313,6 @@
             ex = jnp.exp(sc - jnp.max(sc, axis=-1, keepdims=True))
             probs[lg_i * 4 + h] = ex / jnp.sum(ex, axis=-1, keepdims=True)
 
-    @pl.loop(0, 2)
-    def _(g):
-        for s in range(4):
-            frm = g * 4 + s
-
-            @pl.when(frm != me_yc)
-            def _():
-                remote(
-                    send_rows.at[frm], recv_rows.at[frm], d_ss.at[frm], d_rs.at[frm],
-                    zhi * NYC + frm, me_s,
-                ).wait()
-
-        for p in range(2):
-            grp = 2 * p + g
-            block = recv_rows[pl.ds(g * 4, 4), p].reshape(TOK, C)
-            rows_all[mx, grp] = dot(perm_s[...], block).astype(BF16).reshape(2, 2, 48, C)
-            for which, dev in ((0, dev_x1), (1, dev_x3)):
-                remote(
-                    rows_all.at[mx, grp], rows_all.at[mx, grp], g_ss.at[which, grp],
-                    g_rs.at[which, grp], me_e, dev,
-                ).start()
-
-    forward_weights(1)
-    w_all[zr, 0] = up_ref[...]
-    w_all[zr, 1] = down_ref[...]
-
     def x_recv(which, grp):
         frm, dev = ((x1, dev_x1), (x3, dev_x3))[which]
         return remote(
@@ -300,11 +323,9 @@
     fwd_x = []
 
     def forward_rows(grp):
-        which = 0 if grp < 2 else 1
-        x_recv(which, grp).wait_recv()
-        frm, dev = ((x1, dev_x3), (x3, dev_x1))[which]
+        x_recv(0, grp).wait_recv()
         cp = remote(
-            rows_all.at[frm, grp], rows_all.at[frm, grp], g_ss.at[2, grp], g_rs.at[2, grp], me_e, dev
+            rows_all.at[x1, grp], rows_all.at[x1, grp], g_ss.at[2, grp], g_rs.at[2, grp], me_e, dev_x3
         )
         cp.start()
         fwd_x.append(cp)
@@ -314,52 +335,46 @@
     forward_weights(2)
     forward_rows(1)
     forward_rows(3)
-    forward_weights(3)
-    for way in range(2):
-        for j in range(2):
-            weight_arrived(way, 3, way, j)
-    for grp in (2, 3):
-        x_recv(0, grp).wait_recv()
-    for grp in (0, 1):
+    for grp in range(4):
         x_recv(1, grp).wait_recv()
     for cp in fwd_x:
         cp.wait_recv()
 
-    def expert_rows(p):
-        for m, j in pieces:
-            wcat[m, j] = jnp.concatenate([w_all[p * NZ + c, m, j] for c in range(NZ)], axis=1)
-        for j in range(2):
-            xn = rows_all[:, pl.ds(2 * p, 2), 0, j].reshape(384, C)
-            xsc = rows_all[:, pl.ds(2 * p, 2), 1, j].reshape(384, C)
-            pre = dot(xn, wcat[0, j])
-            sq = pre * pre
-            t = jnp.tanh(GELU_C * pre * (1.0 + GELU_A * sq))
-            act = (0.5 * pre * (1.0 + t)).astype(BF16)
-            slope = 0.5 * (1.0 + t) + 0.5 * GELU_C * pre * (1.0 - t * t) * (1.0 + 3.0 * GELU_A * sq)
-            dact = dot(xsc, wcat[1, j])
-            dsum = jnp.sum(act.astype(F32) * dact, axis=-1, keepdims=True)
-            pg = (dact * slope).astype(BF16)
-            act_s[j] = act
-            pg_s[j] = pg
-            rg = dot_nt(pg, wcat[0, j])
-            part[:, pl.ds(2 * p, 2), pl.ds(j * 48, 48), :] = rg.reshape(4, 2, 48, C)
-            hit = iota((48, C), 1) == iota((48, C), 0) + j * 48
-            for b in range(NX):
-                for g in range(2):
-                    lo = (2 * b + g) * 48
-                    line = jnp.sum(jnp.where(hit, dsum[lo : lo + 48], 0.0), axis=0, keepdims=True)
-                    tail = jnp.where(iota((16, C), 0) == 0, line, 0.0)
-                    if j == 0:
-                        part[b, 2 * p + g, pl.ds(96, 16), :] = tail
-                    else:
-                        part[b, 2 * p + g, pl.ds(96, 16), :] += tail
-
-    def expert_grads(p):
-        for m, j in pieces:
-            left = rows_all[:, pl.ds(2 * p, 2), m, j].reshape(384, C)
-            full = dot_tn(left, (pg_s, act_s)[m][j])
-            for c in range(NZ):
-                grads[p * NZ + c, m, j] = full[:, c * HID : (c + 1) * HID]
+    def rows_of(p, a):
+        return rows_all[:, pl.ds(2 * p, 2), a].reshape(384, C)
+
+    def slice_of(c, m):
+        return jnp.concatenate([w_all[c, m, 0], w_all[c, m, 1]], axis=1)
+
+    def expert_slice(c):
+        p = c // NZ
+        xn = rows_of(p, 0)
+        xsc = rows_of(p, 1)
+        pre = dot(xn, slice_of(c, 0))
+        sq = pre * pre
+        t = jnp.tanh(GELU_C * pre * (1.0 + GELU_A * sq))
+        act = (0.5 * pre * (1.0 + t)).astype(BF16)
+        slope = 0.5 * (1.0 + t) + 0.5 * GELU_C * pre * (1.0 - t * t) * (1.0 + 3.0 * GELU_A * sq)
+        dact = dot(xsc, slice_of(c, 1))
+        dots_s[c] = jnp.sum(act.astype(F32) * dact, axis=-1, keepdims=True)
+        pg = (dact * slope).astype(BF16)
+        pg_s[c] = pg
+        grads[c, 0] = dot_tn(pg, xn).reshape(2, HID, C)
+        grads[c, 1] = dot_tn(act, xsc).reshape(2, HID, C)
+
+    def row_grads(p):
+        pg = jnp.concatenate([pg_s[p * NZ + c] for c in range(NZ)], axis=1)
+        up = jnp.concatenate([slice_of(p * NZ + c, 0) for c in range(NZ)], axis=1)
+        part[:, pl.ds(2 * p, 2), pl.ds(0, 48), :] = dot_nt(pg, up).reshape(4, 2, 48, C)
+        dsum = dots_s[p * NZ]
+        for c in range(1, NZ):
+            dsum = dsum + dots_s[p * NZ + c]
+        hit = iota((48, C), 1) == iota((48, C), 0)
+        for b in range(NX):
+            for g in range(2):
+                lo = (2 * b + g) * 48
+                line = jnp.sum(jnp.where(hit, dsum[lo : lo + 48], 0.0), axis=0, keepdims=True)
+                part[b, 2 * p + g, pl.ds(48, 16), :] = jnp.where(iota((16, C), 0) == 0, line, 0.0)
 
     def x_send(n, dev, slot, sem):
         return remote(xs.at[n], xr.at[slot], x_ss.at[n], x_rs.at[sem], me_e, dev)
@@ -393,41 +408,55 @@
         sums.append(x_send(slot, dev, slot, slot))
         sums[-1].start()
 
-    expert_rows(1 - zhi)
-    expert_grads(1 - zhi)
-    for m, j in pieces:
+    def away(n):
+        return (zr + n + RING) % RING
+
+    for n in (0, 1, -1):
+        expert_slice(away(n))
+    forward_weights(3)
+    expert_slice(away(3))
+    for j in (1, 0):
+        start_sum(0, 1, 1, j, False)
+    expert_slice(away(-3))
+    for j in (1, 0):
+        start_sum(1, 1, 0, j, False)
+    expert_slice(away(2))
+    expert_slice(away(-2))
+    for way in range(2):
+        for j in range(2):
+            weight_arrived(way, 3, way, j)
+    expert_slice(away(4))
+    turn = [(m, j) for j in (1, 0) for m in range(2)]
+    for m, j in turn:
         start_sum(m, 0, m, j, False)
-    expert_rows(zhi)
-    for g in (0, 1):
-        send_sum(8 + g, dev_x1, part[x2, g])
-        send_sum(10 + g, dev_x3, part[x2, 2 + g])
-    for g in (0, 1):
-        send_sum(g, dev_x1, part[x1, g])
-        send_sum(6 + g, dev_x3, part[x3, 2 + g])
-    expert_grads(zhi)
-    for m, j in pieces:
-        start_sum(1 - m, 1, m, j, False)
-    for m, j in pieces:
+    row_grads(1 - zhi)
+    row_grads(zhi)
+    for grp in range(4):
+        send_sum(grp, dev_x3, part[x2, grp])
+    for grp in range(4):
+        send_sum(4 + grp, dev_x3, part[x3, grp])
+    for m, j in turn:
         start_sum(m, 1, m, j, True)
-    for g in (0, 1):
-        x_got(8 + g).wait_recv()
-        send_sum(4 + g, dev_x3, part[x3, g] + xr[8 + g].astype(F32))
-        x_got(10 + g).wait_recv()
-        send_sum(2 + g, dev_x1, part[x1, 2 + g] + xr[10 + g].astype(F32))
-
-    ro = iota((128, 112), 0)
+    for grp in (0, 2, 1, 3):
+        x_got(grp).wait_recv()
+        send_sum(8 + grp, dev_x1, part[x1, grp] + xr[grp].astype(F32))
+
+    ro = iota((128, 128), 0)
     rs = ge(ro, 32) + ge(ro, 64) + ge(ro, 96)
     rq = ro - 32 * rs
     rj = ge(rq, 12)
-    want = jnp.where(rq < 24, rj * 48 + rs * 12 + rq - 12 * rj, jnp.where(rq < 26, rq + 72, -1))
-    back = ones_where(iota((128, 112), 1) == want)
+    half_of = jnp.where(rj == mine, 0, 64)
+    want = half_of + rs * 12 + rq - 12 * rj
+    want = jnp.where(rq < 24, want, jnp.where(rq < 26, rq + 24, jnp.where(rq < 28, rq + 86, -1)))
+    back = ones_where(iota((128, 128), 1) == want)
     for g in range(2):
         for p in range(2):
             grp = 2 * p + g
-            x_got(grp).wait_recv()
             x_got(4 + grp).wait_recv()
-            total = split_tail(part[mx, grp] + xr[grp].astype(F32) + xr[4 + grp].astype(F32))
-            ret_send[pl.ds(g * 4, 4), p] = dot(back, total).astype(BF16).reshape(4, 32, C)
+            x_got(8 + grp).wait_recv()
+            total = split_tail(part[mx, grp] + xr[4 + grp].astype(F32))
+            both = jnp.concatenate([total, xr[8 + grp]], axis=0)
+            ret_send[pl.ds(g * 4, 4), p] = dot(back, both).astype(BF16).reshape(4, 32, C)
         for s in range(4):
             to = g * 4 + s
 
@@ -439,7 +468,7 @@
                 ).start()
 
     ret_recv[me_yc] = ret_send[me_yc]
-    for m, j in pieces:
+    for m, j in turn:
         for way in range(2):
             start_sum(way, 2, m, j, True)
 
@@ -477,8 +506,9 @@
     cot = cot_s[...].astype(F32)
     res_grad = (cot + (norm_grad - nf * inner) / rms).astype(BF16)
     stage[...] = res_grad
-    gsend[...] = stage[pl.ds(0, HALF), :]
-    halo_g = remote(gsend, gw.at[1], h_ss.at[1], h_rs.at[1], me_e, before)
+    pack_one = packing(1, 80)
+    gsend[...] = dot(pack_one, stage[pl.ds(0, HALF), :]).astype(BF16)
+    halo_g = remote(gsend, grecv, h_ss.at[1], h_rs.at[1], me_e, before)
     halo_g.start()
     gw[0] = stage[pl.ds(HALF, HALF), :]
     for r in range(WIN):
@@ -487,13 +517,13 @@
     gate1, gate2 = cols[:, 0:1], cols[:, 1:2]
     keep1, keep2 = cols[:, 3:4], cols[:, 4:5]
     narrow = returned[:, :128]
-    tail_pos = (pos == 24) | (pos == 25)
 
     def gathered(idk, slotk):
         half = lax.shift_right_arithmetic(idk, 1)
-        pickk = ones_where((dev == half) & tail_pos)
+        line = jnp.where(idk - 2 * half == mine, 24, 26)
+        pickk = ones_where((dev == half) & ((pos == line) | (pos == line + 1)))
         found = dot(pickk, narrow)
-        spot = (idk - 2 * half) * 48 + (me_e % 4) * 12 + slotk
+        spot = (me_e % 4) * 12 + slotk
         return jnp.sum(jnp.where(iota((TOK, 128), 1) == spot, found, 0.0), axis=-1, keepdims=True)
 
     d1 = gathered(id1, slot1)
@@ -508,11 +538,12 @@
     for r in range(WIN):
         logit_out[r] = lg_s[pl.ds(r * PADW, WIN), :]
 
-    for m, j in pieces:
+    for m, j in turn:
         for way in range(2):
             start_sum(way, 3, m, j, True)
 
     halo_g.wait_recv()
+    gw[1] = dot_tn(pack_one, grecv[...]).astype(BF16)
 
     @pl.loop(0, 4)
     def _(lg_i):
@@ -539,15 +570,16 @@
         agrad[1, :, lanes] = (dk * inv_sqrt).astype(BF16)
         agrad[2, :, lanes] = dv.astype(BF16)
 
-    asend[...] = agrad[:, pl.ds(HALF, HALF), :]
+    asend[...] = dot(pack_s[...], agrad[:, pl.ds(HALF, HALF), :].reshape(3 * HALF, C)).astype(BF16)
     halo_a = remote(asend, arecv, h_ss.at[2], h_rs.at[2], me_e, after)
     halo_a.start()
     for r in range(half_rows):
         for k in range(3):
             attn_out[k, half_rows + r] = agrad[k, pl.ds(r * PADW, WIN), :]
 
-    for m, out in ((0, up_out), (1, down_out)):
-        for j in range(2):
+    swap_g = []
+    for j in (1, 0):
+        for m, out in ((0, up_out), (1, down_out)):
             value = grads[zr, m, j]
             for way in range(2):
                 remote(
@@ -555,14 +587,24 @@
                     z_rs.at[way, 3, m, j], *ring[way],
                 ).wait_recv()
                 value = value + zrecv[way, 3, m, j].astype(F32)
-            out[j] = value
+            if j == 1:
+                gswap[0, m] = value.astype(BF16)
+                cp = remote(gswap.at[0, m], gswap.at[1, m], s_ss.at[2 + m], s_rs.at[2 + m], me_e, dev_x1)
+                cp.start()
+                swap_g.append(cp)
+            else:
+                out[mine] = value.T
+    for m, out in ((0, up_out), (1, down_out)):
+        swap_g[m].wait_recv()
+        out[other] = gswap[1, m].astype(F32).T
 
     halo_a.wait_recv()
+    qw[1] = dot_tn(pack_s[...], arecv[...]).astype(BF16).reshape(3, HALF, C)
     for r in range(half_rows):
         for k in range(3):
-            attn_out[k, r] = arecv[k, pl.ds(r * PADW, WIN), :]
-
-    for cp in (*sent_w, *fwd_x, *sums, *sent_z, halo_q, halo_g, halo_a):
+            attn_out[k, r] = qw[1, k, pl.ds(r * PADW, WIN), :]
+
+    for cp in (*sent_w, *swap_w, *fwd_x, *sums, *sent_z, *swap_g, halo_q, halo_g, halo_a):
         cp.wait_send()
     for grp in range(4):
         for which in range(2):
@@ -585,12 +627,15 @@
         out_specs=(vmem,) * 5,
         scratch_shapes=[
             pltpu.VMEM((2, 3, HALF, C), BF16),
-            pltpu.VMEM((3, HALF, C), BF16),
+            pltpu.VMEM((224, C), BF16),
+            pltpu.VMEM((224, C), BF16),
+            pltpu.VMEM((224, 3 * HALF), BF16),
             pltpu.VMEM((2, HALF, C), BF16),
-            pltpu.VMEM((HALF, C), BF16),
+            pltpu.VMEM((80, C), BF16),
+            pltpu.VMEM((80, C), BF16),
             pltpu.VMEM((3, TOK, C), BF16),
-            pltpu.VMEM((3, HALF, C), BF16),
-            pltpu.VMEM((3, HALF, C), BF16),
+            pltpu.VMEM((224, C), BF16),
+            pltpu.VMEM((224, C), BF16),
             pltpu.VMEM((TOK, C), BF16),
             pltpu.VMEM((TOK, C), BF16),
             pltpu.VMEM((TOK, EXPERTS), F32),
@@ -601,21 +646,22 @@
             pltpu.VMEM((HEADS, TOK, TOK), F32),
             pltpu.VMEM((TOK, TOK), BF16),
             pltpu.VMEM((TOK, TOK), F32),
+            pltpu.VMEM((2, 2, HID, C), BF16),
             pltpu.VMEM((NYC, 2, 48, C), BF16),
             pltpu.VMEM((NYC, 2, 48, C), BF16),
-            pltpu.VMEM((NX, 4, 2, 2, 48, C), BF16),
+            pltpu.VMEM((4, 2, 2, 48, C), BF16),
+            pltpu.VMEM((NX, 4, 2, 48, C), BF16),
             pltpu.VMEM((RING, 2, 2, C, HID), BF16),
-            pltpu.VMEM((2, 2, C, NZ * HID), BF16),
-            pltpu.VMEM((2, 384, NZ * HID), BF16),
-            pltpu.VMEM((2, 384, NZ * HID), BF16),
-            pltpu.VMEM((NX, 4, 112, C), F32),
-            pltpu.VMEM((12, 112, C), BF16),
-            pltpu.VMEM((12, 112, C), BF16),
+            pltpu.VMEM((RING, 384, 2 * HID), BF16),
+            pltpu.VMEM((RING, 384, 1), F32),
+            pltpu.VMEM((NX, 4, 64, C), F32),
+            pltpu.VMEM((12, 64, C), BF16),
+            pltpu.VMEM((12, 64, C), BF16),
             pltpu.VMEM((NYC, 2, 32, C), BF16),
             pltpu.VMEM((NYC, 2, 32, C), BF16),
-            pltpu.VMEM((RING, 2, 2, C, HID), F32),
-            pltpu.VMEM((2, 4, 2, 2, C, HID), BF16),
-            pltpu.VMEM((2, 4, 2, 2, C, HID), BF16),
+            pltpu.VMEM((RING, 2, 2, HID, C), F32),
+            pltpu.VMEM((2, 4, 2, 2, HID, C), BF16),
+            pltpu.VMEM((2, 4, 2, 2, HID, C), BF16),
             dma((NYC,)), dma((NYC,)),
             dma((3, 4)), dma((3, 4)),
             dma((2, 4, 2, 2)), dma((2, 4, 2, 2)),
@@ -623,6 +669,7 @@
             dma((NYC,)), dma((NYC,)),
             dma((2, 4, 2, 2)), dma((2, 4, 2, 2)),
             dma((3,)), dma((3,)),
+            dma((4,)), dma((4,)),
         ],
         compiler_params=pltpu.CompilerParams(
             collective_id=0, has_side_effects=True, vmem_limit_bytes=56 * 1024 * 1024

time: 130 us -> 124 us (0.954); the launches traced: 128 us -> 124 us
  Pallas kernels: 118 us -> 114 us
    pallas_call x1, Pallas kernels: 118 us -> 114 us  [per_device(): pl.pallas_call(kernel, out_shape=(jax.ShapeDtypeStruct((3, WIN, WIN, C),...]
where the time goes in v4:
time: 124 us
  Pallas kernels  114 us (92%)
  local copies, waits for them, and re-layouts  9.43 us (8%)
    pallas_call x1, Pallas kernels, per_device(): pl.pallas_call(kernel, out_shape=(jax.ShapeDtypeStruct((3, WIN, WIN, C),...  114 us
    unnamed x18, local copies, waits for them, and re-layouts  9.43 us

profile of v4, /device:TPU:24, one launch (start us, length us, event | category | flops | bytes accessed | tf_op | source)
XLA Modules:
  0.0 123.9 jit_solution(16653782750375873350)
XLA Ops:
  0.6 0.0 copy-start.3
  0.6 1.5 %copy.19 = f32[1,12,12,32]{3,2,0,1:T(8,128)} copy(f32[1,12,12,32]{3,0,2,1:T(1,128)} %param.10) | data formatting | bytes 36864
  2.2 0.0 copy-done.3
  2.2 0.0 copy-start.4
  2.2 0.8 copy.13
  3.0 0.0 copy-done.4
  3.0 0.8 copy.14
  3.8 113.8 %shard_map.119 = (bf16[3,12,12,512]{3,2,1,0:T(8,128)(2,1)}, bf16[12,12,512]{2,1,0:T(8,128)(2,1)}, f32[2,512,128]{2,1,0:T(8,128)}, f32[2,512,128]{2,1,0:T(8,128)}, f32[12,12,32]{2,1,0:T(8,128)}) custom-call(bf16[3,12,12,512]{3,2,1,0:T(8,128)(2,1)} %bitcast.13, bf16[12,12,512]{2,1,0:T(8,128)(2,1)} %bitcast.18, f32[12,12,32]{2,1,0:T(8,128)} %bitcast.17, ...), custom_call_target="tpu_custom_call" | custom-call | tf_op jit(solution)/shard_map/pallas_call | solution.py:617
  117.6 1.6 %copy.16 = f32[1,12,12,32]{3,0,2,1:T(1,128)} copy(f32[1,12,12,32]{3,2,1,0:T(8,128)} %bitcast.21) | data formatting | bytes 36864
  119.2 0.0 copy-start.2
  119.2 0.0 copy-start.1
  119.2 2.0 %copy.24 = bf16[3,1,12,12,512]{4,3,2,1,0:T(8,128)(2,1)} copy(bf16[3,1,12,12,512]{4,3,2,1,0:T(8,128)(2,1)} %bitcast.14) | data formatting | bytes 884736
  121.2 0.0 copy-done.2
  121.2 0.7 copy.25
  121.9 0.0 copy-done.1
  121.9 0.0 copy-start
  121.9 0.8 copy.26
  122.7 0.4 copy-done
  123.1 0.8 copy.27
Async XLA Ops:
  0.6 1.5 %copy-start.3 = (s32[1,12,12,2]{2,3,1,0:T(2,128)S(1)}, s32[1,12,12,2]{2,3,1,0:T(2,128)}, u32[]{:S(2)}) copy-start(s32[1,12,12,2]{2,3,1,0:T(2,128)} %param.11) | copy-start | bytes 3460
  2.2 0.8 copy-start.4
  119.2 2.0 %copy-start.2 = (bf16[12,12,512]{2,1,0:T(8,128)(2,1)S(1)}, bf16[12,12,512]{2,1,0:T(8,128)(2,1)}, u32[]{:S(2)}) copy-start(bf16[12,12,512]{2,1,0:T(8,128)(2,1)} %get-tuple-element.11) | copy-start | bytes 442372
  119.2 2.7 %copy-start.1 = (f32[2,512,128]{2,1,0:T(8,128)S(1)}, f32[2,512,128]{2,1,0:T(8,128)}, u32[]{:S(2)}) copy-start(f32[2,512,128]{2,1,0:T(8,128)} %get-tuple-element.27) | copy-start | bytes 1572868
  121.9 1.2 copy-start

commit v5 on v4

--- a/solution.py
+++ b/solution.py
@@ -114,6 +114,46 @@
     for s in (dev_x1, dev_x3, after, before):
         greet(me_e, s)
 
+    pl.semaphore_wait(barrier, NYC - 1 + 6)
+
+    def weight_copy(way, step, m, j):
+        chunk = (zr - step) % RING if way == 0 else (zr + step) % RING
+        src = (up_ref, down_ref)[m].at[mine] if step == 0 and j == 0 else w_all.at[chunk, m, j]
+        return remote(
+            src, w_all.at[chunk, m, j], w_ss.at[way, step, m, j], w_rs.at[way, step, m, j], *ring[way]
+        )
+
+    def weight_arrived(way, step, m, j):
+        chunk = (zr - 1 - step) % RING if way == 0 else (zr + 1 + step) % RING
+        remote(
+            w_all.at[chunk, m, j], w_all.at[chunk, m, j], w_ss.at[way, step, m, j],
+            w_rs.at[way, step, m, j], *ring[way],
+        ).wait_recv()
+
+    pieces = [(m, j) for j in range(2) for m in range(2)]
+    sent_w = []
+
+    def start_weight(way, step, m, j):
+        cp = weight_copy(way, step, m, j)
+        cp.start()
+        sent_w.append(cp)
+
+    def forward_weights(step, j):
+        for m in range(2):
+            for way in range(2):
+                weight_arrived(way, step - 1, m, j)
+                if step < 3 or m == way:
+                    start_weight(way, step, m, j)
+
+    swap_w = [
+        remote((up_ref, down_ref)[m].at[other], w_all.at[zr, m, 1], s_ss.at[m], s_rs.at[m], me_e, dev_x1)
+        for m in range(2)
+    ]
+    for m in range(2):
+        swap_w[m].start()
+        for way in range(2):
+            start_weight(way, 0, m, 0)
+
     half_rows = WIN // 2
     qw[...] = jnp.zeros((2, 3, HALF, C), BF16)
     resid_s[...] = jnp.zeros((TOK, C), BF16)
@@ -125,53 +165,17 @@
         at = pl.ds(r * PADW, WIN)
         resid_s[at, :] = resid_ref[r]
         cot_s[at, :] = cot_ref[r]
-        lg_s[at, :] = logit_ref[r]
-        ids_s[at, :] = ids_ref[r]
-        keep_s[at, :] = keep_ref[r]
+        lg_s[at, :] = logit_ref[pl.ds(r * WIN, WIN), 0, :]
+        for ref, to in ((ids_ref, ids_s), (keep_ref, keep_s)):
+            for k in range(2):
+                line = ref[r, pl.ds(k, 1), :]
+                to[at, pl.ds(k, 1)] = jnp.sum(
+                    jnp.where(iota((WIN, WIN), 0) == iota((WIN, WIN), 1), line, 0), axis=1, keepdims=True
+                )
     for r in range(half_rows):
         for k in range(3):
             qw[1, k, pl.ds(r * PADW, WIN), :] = attn_ref[k, r]
             qw[0, k, pl.ds(r * PADW, WIN), :] = attn_ref[k, half_rows + r]
-
-    pl.semaphore_wait(barrier, NYC - 1 + 6)
-
-    def weight_copy(way, step, m, j):
-        chunk = (zr - step) % RING if way == 0 else (zr + step) % RING
-        src = (up_ref, down_ref)[m].at[mine] if step == 0 and j == 0 else w_all.at[chunk, m, j]
-        return remote(
-            src, w_all.at[chunk, m, j], w_ss.at[way, step, m, j], w_rs.at[way, step, m, j], *ring[way]
-        )
-
-    def weight_arrived(way, step, m, j):
-        chunk = (zr - 1 - step) % RING if way == 0 else (zr + 1 + step) % RING
-        remote(
-            w_all.at[chunk, m, j], w_all.at[chunk, m, j], w_ss.at[way, step, m, j],
-            w_rs.at[way, step, m, j], *ring[way],
-        ).wait_recv()
-
-    pieces = [(m, j) for j in range(2) for m in range(2)]
-    sent_w = []
-
-    def start_weight(way, step, m, j):
-        cp = weight_copy(way, step, m, j)
-        cp.start()
-        sent_w.append(cp)
-
-    def forward_weights(step):
-        for m, j in pieces:
-            for way in range(2):
-                weight_arrived(way, step - 1, m, j)
-                if step < 3 or m == way:
-                    start_weight(way, step, m, j)
-
-    swap_w = [
-        remote((up_ref, down_ref)[m].at[other], w_all.at[zr, m, 1], s_ss.at[m], s_rs.at[m], me_e, dev_x1)
-        for m in range(2)
-    ]
-    for m in range(2):
-        swap_w[m].start()
-        for way in range(2):
-            start_weight(way, 0, m, 0)
 
     def packing(count, dense):
         wide, narrow = count * HALF, dense
@@ -219,11 +223,6 @@
         column = jnp.where(lane == i, v, column)
     cols[...] = column
 
-    for m in range(2):
-        swap_w[m].wait_recv()
-        for way in range(2):
-            start_weight(way, 0, m, 1)
-
     row = iota((TOK, 1), 0)
     src4 = ge(row, 48) + ge(row, 96) + ge(row, 144)
     rem = row - 48 * src4
@@ -251,6 +250,10 @@
                 ).start()
 
     recv_rows[me_yc] = send_rows[me_yc]
+    for m in range(2):
+        swap_w[m].wait_recv()
+        for way in range(2):
+            start_weight(way, 0, m, 1)
 
     b96 = ge(row, 96)
     o2 = row - 96 * b96
@@ -258,6 +261,8 @@
     o3 = o2 - 48 * b48
     s12 = ge(o3, 12) + ge(o3, 24) + ge(o3, 36)
     perm_s[...] = ones_where(square_c == s12 * 48 + b48 * 24 + b96 * 12 + (o3 - 12 * s12))
+
+    forward_weights(1, 0)
 
     @pl.loop(0, 2)
     def _(g):
@@ -282,7 +287,7 @@
                 ).start()
             rows_all[mx, grp] = rows_two[grp, mine]
 
-    forward_weights(1)
+    forward_weights(1, 1)
     w_all[zr, 0, 0] = up_ref[mine]
     w_all[zr, 1, 0] = down_ref[mine]
 
@@ -332,9 +337,12 @@
 
     forward_rows(0)
     forward_rows(2)
-    forward_weights(2)
+    forward_weights(2, 0)
     forward_rows(1)
     forward_rows(3)
+    forward_weights(2, 1)
+    forward_weights(3, 0)
+    forward_weights(3, 1)
     for grp in range(4):
         x_recv(1, grp).wait_recv()
     for cp in fwd_x:
@@ -411,17 +419,19 @@
     def away(n):
         return (zr + n + RING) % RING
 
-    for n in (0, 1, -1):
-        expert_slice(away(n))
-    forward_weights(3)
     expert_slice(away(3))
     for j in (1, 0):
         start_sum(0, 1, 1, j, False)
     expert_slice(away(-3))
     for j in (1, 0):
         start_sum(1, 1, 0, j, False)
-    expert_slice(away(2))
-    expert_slice(away(-2))
+    for n in (0, 1, -1, 2, -2):
+        expert_slice(away(n))
+    row_grads(zhi)
+    for g in range(2):
+        send_sum(2 * zhi + g, dev_x3, part[x2, 2 * zhi + g])
+    for g in range(2):
+        send_sum(4 + 2 * zhi + g, dev_x3, part[x3, 2 * zhi + g])
     for way in range(2):
         for j in range(2):
             weight_arrived(way, 3, way, j)
@@ -429,17 +439,26 @@
     turn = [(m, j) for j in (1, 0) for m in range(2)]
     for m, j in turn:
         start_sum(m, 0, m, j, False)
-    row_grads(1 - zhi)
-    row_grads(zhi)
-    for grp in range(4):
-        send_sum(grp, dev_x3, part[x2, grp])
-    for grp in range(4):
-        send_sum(4 + grp, dev_x3, part[x3, grp])
+    far = 1 - zhi
+    row_grads(far)
+    for g in range(2):
+        send_sum(2 * far + g, dev_x3, part[x2, 2 * far + g])
+    for g in range(2):
+        send_sum(4 + 2 * far + g, dev_x3, part[x3, 2 * far + g])
+
+    def relay(grp):
+        x_got(grp).wait_recv()
+        send_sum(8 + grp, dev_x1, part[x1, grp] + xr[grp].astype(F32))
+
+    for g in range(2):
+        relay(2 * zhi + g)
     for m, j in turn:
         start_sum(m, 1, m, j, True)
-    for grp in (0, 2, 1, 3):
-        x_got(grp).wait_recv()
-        send_sum(8 + grp, dev_x1, part[x1, grp] + xr[grp].astype(F32))
+    for g in range(2):
+        relay(2 * far + g)
+    for j in (1, 0):
+        for way in range(2):
+            start_sum(way, 2, 1 - way, j, True)
 
     ro = iota((128, 128), 0)
     rs = ge(ro, 32) + ge(ro, 64) + ge(ro, 96)
@@ -468,9 +487,9 @@
                 ).start()
 
     ret_recv[me_yc] = ret_send[me_yc]
-    for m, j in turn:
+    for j in (1, 0):
         for way in range(2):
-            start_sum(way, 2, m, j, True)
+            start_sum(way, 2, way, j, True)
 
     @pl.loop(0, NYC)
     def _(frm):
@@ -480,6 +499,10 @@
                 ret_send.at[frm], ret_recv.at[frm], r_ss.at[frm], r_rs.at[frm],
                 zhi * NYC + frm, me_s,
             ).wait()
+
+    for j in (1, 0):
+        for way in range(2):
+            start_sum(way, 3, 1 - way, j, True)
 
     returned = ret_recv[...].reshape(NE * 32, C)
     ids = ids_s[...]
@@ -536,11 +559,11 @@
     share_mean = jnp.sum(rp * share, axis=-1, keepdims=True)
     lg_s[...] = (oh1 - oh2) * part1 + EXPERTS * rp * (share - share_mean)
     for r in range(WIN):
-        logit_out[r] = lg_s[pl.ds(r * PADW, WIN), :]
-
-    for m, j in turn:
+        logit_out[pl.ds(r * WIN, WIN), 0, :] = lg_s[pl.ds(r * PADW, WIN), :]
+
+    for j in (1, 0):
         for way in range(2):
-            start_sum(way, 3, m, j, True)
+            start_sum(way, 3, way, j, True)
 
     halo_g.wait_recv()
     gw[1] = dot_tn(pack_one, grecv[...]).astype(BF16)
@@ -611,6 +634,11 @@
             x_recv(which, grp).wait_send()
 
 
+def move_out(*refs):
+    for i in range(5):
+        refs[5 + i][...] = refs[i][...]
+
+
 def per_device(attn_inputs, residual, logits, expert_ids, keep_mask, cotangent, up_weight, down_weight):
     vmem = pl.BlockSpec(memory_space=pltpu.VMEM)
     dma = pltpu.SemaphoreType.DMA
@@ -621,7 +649,7 @@
             jax.ShapeDtypeStruct((WIN, WIN, C), BF16),
             jax.ShapeDtypeStruct((2, C, HID), F32),
             jax.ShapeDtypeStruct((2, C, HID), F32),
-            jax.ShapeDtypeStruct((WIN, WIN, EXPERTS), F32),
+            jax.ShapeDtypeStruct((WIN * WIN, 1, EXPERTS), F32),
         ),
         in_specs=[vmem] * 8,
         out_specs=(vmem,) * 5,
@@ -675,11 +703,21 @@
             collective_id=0, has_side_effects=True, vmem_limit_bytes=56 * 1024 * 1024
         ),
     )(
-        attn_inputs[:, 0], residual[0], logits[0], expert_ids[0], keep_mask[0], cotangent[0],
+        attn_inputs[:, 0], residual[0], logits.reshape(WIN * WIN, 1, EXPERTS),
+        jnp.swapaxes(expert_ids[0], 1, 2), jnp.swapaxes(keep_mask[0], 1, 2), cotangent[0],
         up_weight, down_weight,
     )
+    outs = pl.pallas_call(
+        move_out,
+        out_shape=tuple(jax.ShapeDtypeStruct(o.shape, o.dtype) for o in outs),
+        in_specs=[vmem] * 5,
+        out_specs=(vmem,) * 5,
+    )(*outs)
     attn_grad, res_grad, up_grad, down_grad, logit_grad = outs
-    return attn_grad[:, None], res_grad[None], up_grad, down_grad, logit_grad[None]
+    return (
+        attn_grad[:, None], res_grad[None], up_grad, down_grad,
+        logit_grad.reshape(1, WIN, WIN, EXPERTS),
+    )
 
 
 def solution(mesh):

time: 124 us -> 113 us (0.911)
  local copies, waits for them, and re-layouts: 9.43 us -> 0 us
  Pallas kernels: 114 us -> 112 us
    unnamed x18 -> x0, local copies, waits for them, and re-layouts: 9.43 us -> none
    pallas_call x1, Pallas kernels: 114 us -> 109 us  [per_device(): pl.pallas_call(kernel, out_shape=(jax.ShapeDtypeStruct((3, WIN, WIN, C),...]
    pallas_call x0 -> x1, Pallas kernels: none -> 2.74 us  [per_device(): pl.pallas_call(move_out, out_shape=tuple((jax.ShapeDtypeStruct(o.shape, o...]
where the time goes in v5:
time: 113 us
  Pallas kernels  112 us (99%)
    pallas_call x1, Pallas kernels, per_device(): pl.pallas_call(kernel, out_shape=(jax.ShapeDtypeStruct((3, WIN, WIN, C),...  109 us
    pallas_call x1, Pallas kernels, per_device(): pl.pallas_call(move_out, out_shape=tuple((jax.ShapeDtypeStruct(o.shape, o...  2.74 us

profile of v5, /device:TPU:24, one launch (start us, length us, event | category | flops | bytes accessed | tf_op | source)
XLA Modules:
  0.0 112.7 jit_solution(18093776378511380629)
XLA Ops:
  0.6 109.4 %shard_map.119 = (bf16[3,12,12,512]{3,2,1,0:T(8,128)(2,1)}, bf16[12,12,512]{2,1,0:T(8,128)(2,1)}, f32[2,512,128]{2,1,0:T(8,128)}, f32[2,512,128]{2,1,0:T(8,128)}, f32[144,1,32]{2,1,0:T(1,128)}) custom-call(bf16[3,12,12,512]{3,2,1,0:T(8,128)(2,1)} %bitcast.15, bf16[12,12,512]{2,1,0:T(8,128)(2,1)} %bitcast.16, f32[144,1,32]{2,1,0:T(1,128)} %bitcast.18, ...), custom_call_target="tpu_custom_call" | custom-call | tf_op jit(solution)/shard_map/pallas_call | solution.py:645
  110.0 2.7 %shard_map.120 = (bf16[3,12,12,512]{3,2,1,0:T(8,128)(2,1)}, bf16[12,12,512]{2,1,0:T(8,128)(2,1)}, f32[2,512,128]{2,1,0:T(8,128)}, f32[2,512,128]{2,1,0:T(8,128)}, f32[144,1,32]{2,1,0:T(1,128)}) custom-call(bf16[3,12,12,512]{3,2,1,0:T(8,128)(2,1)} %get-tuple-element.15.refs_0_, bf16[12,12,512]{2,1,0:T(8,128)(2,1)} %get-tuple-element.16.refs_1_, ...), custom_call_target="tpu_custom_call" | custom-call | tf_op jit(solution)/shard_map/pallas_call | solution.py:710

commit v6 on v5

--- a/solution.py
+++ b/solution.py
@@ -63,11 +63,11 @@
 
 
 def kernel(
-    attn_ref, resid_ref, logit_ref, ids_ref, keep_ref, cot_ref, up_ref, down_ref,
+    attn_hbm, resid_hbm, logit_ref, ids_ref, keep_ref, cot_hbm, up_ref, down_ref,
     attn_out, res_out, up_out, down_out, logit_out,
     qw, qsend, qrecv, pack_s, gw, gsend, grecv, agrad, asend, arecv,
     resid_s, cot_s, lg_s, ids_s, keep_s, cols, stage, probs, perm_s, bias_s,
-    gswap, send_rows, recv_rows, rows_two, rows_all, w_all, pg_s, dots_s, part, xs, xr,
+    attn_ref, resid_ref, cot_ref, in_sem, gswap, send_rows, recv_rows, rows_two, rows_all, w_all, pg_s, dots_s, part, xs, xr,
     ret_send, ret_recv, grads, zsend, zrecv,
     d_ss, d_rs, g_ss, g_rs, w_ss, w_rs, x_ss, x_rs, r_ss, r_rs, z_ss, z_rs, h_ss, h_rs, s_ss, s_rs,
 ):
@@ -98,6 +98,14 @@
             device_id={"expert": e, "space": s}, device_id_type=pl.DeviceIdType.MESH,
         )
 
+    fetched = [
+        pltpu.make_async_copy(src, dst, in_sem.at[i])
+        for i, (src, dst) in enumerate(
+            ((attn_hbm, attn_ref), (resid_hbm, resid_ref), (cot_hbm, cot_ref))
+        )
+    ]
+    for cp in fetched:
+        cp.start()
     barrier = pltpu.get_barrier_semaphore()
 
     def greet(e, s):
@@ -161,6 +169,8 @@
     lg_s[...] = jnp.zeros((TOK, EXPERTS), F32)
     ids_s[...] = jnp.full((TOK, 2), -1, I32)
     keep_s[...] = jnp.zeros((TOK, 2), I32)
+    for cp in fetched:
+        cp.wait()
     for r in range(WIN):
         at = pl.ds(r * PADW, WIN)
         resid_s[at, :] = resid_ref[r]
@@ -635,12 +645,21 @@
 
 
 def move_out(*refs):
+    held, sems = refs[10:15], refs[15]
+    reads = [pltpu.make_async_copy(refs[i], held[i], sems.at[0, i]) for i in range(5)]
+    writes = [pltpu.make_async_copy(held[i], refs[5 + i], sems.at[1, i]) for i in range(5)]
+    for cp in reads:
+        cp.start()
     for i in range(5):
-        refs[5 + i][...] = refs[i][...]
+        reads[i].wait()
+        writes[i].start()
+    for cp in writes:
+        cp.wait()
 
 
 def per_device(attn_inputs, residual, logits, expert_ids, keep_mask, cotangent, up_weight, down_weight):
     vmem = pl.BlockSpec(memory_space=pltpu.VMEM)
+    anywhere = pl.BlockSpec(memory_space=pl.ANY)
     dma = pltpu.SemaphoreType.DMA
     outs = pl.pallas_call(
         kernel,
@@ -651,7 +670,7 @@
             jax.ShapeDtypeStruct((2, C, HID), F32),
             jax.ShapeDtypeStruct((WIN * WIN, 1, EXPERTS), F32),
         ),
-        in_specs=[vmem] * 8,
+        in_specs=[anywhere, anywhere, vmem, vmem, vmem, anywhere, vmem, vmem],
         out_specs=(vmem,) * 5,
         scratch_shapes=[
             pltpu.VMEM((2, 3, HALF, C), BF16),
@@ -674,6 +693,10 @@
             pltpu.VMEM((HEADS, TOK, TOK), F32),
             pltpu.VMEM((TOK, TOK), BF16),
             pltpu.VMEM((TOK, TOK), F32),
+            pltpu.VMEM((3, WIN, WIN, C), BF16),
+            pltpu.VMEM((WIN, WIN, C), BF16),
+            pltpu.VMEM((WIN, WIN, C), BF16),
+            dma((3,)),
             pltpu.VMEM((2, 2, HID, C), BF16),
             pltpu.VMEM((NYC, 2, 48, C), BF16),
             pltpu.VMEM((NYC, 2, 48, C), BF16),
@@ -710,8 +733,9 @@
     outs = pl.pallas_call(
         move_out,
         out_shape=tuple(jax.ShapeDtypeStruct(o.shape, o.dtype) for o in outs),
-        in_specs=[vmem] * 5,
-        out_specs=(vmem,) * 5,
+        in_specs=[anywhere] * 5,
+        out_specs=(anywhere,) * 5,
+        scratch_shapes=[pltpu.VMEM(o.shape, o.dtype) for o in outs] + [dma((2, 5))],
     )(*outs)
     attn_grad, res_grad, up_grad, down_grad, logit_grad = outs
     return (

time: 113 us -> 112 us (level)
  no operation moved by 1% of the time
where the time goes in v6:
time: 112 us
  Pallas kernels  111 us (99%)
    pallas_call x1, Pallas kernels, per_device(): pl.pallas_call(kernel, out_shape=(jax.ShapeDtypeStruct((3, WIN, WIN, C),...  109 us
    pallas_call x1, Pallas kernels, per_device(): pl.pallas_call(move_out, out_shape=tuple((jax.ShapeDtypeStruct(o.shape, o...  2.39 us

profile of v6, /device:TPU:24, one launch (start us, length us, event | category | flops | bytes accessed | tf_op | source)
XLA Modules:
  0.0 112.0 jit_solution(6648325500493456179)
XLA Ops:
  0.6 109.0 %shard_map.119 = (bf16[3,12,12,512]{3,2,1,0:T(8,128)(2,1)}, bf16[12,12,512]{2,1,0:T(8,128)(2,1)}, f32[2,512,128]{2,1,0:T(8,128)}, f32[2,512,128]{2,1,0:T(8,128)}, f32[144,1,32]{2,1,0:T(1,128)}) custom-call(bf16[3,12,12,512]{3,2,1,0:T(8,128)(2,1)} %bitcast.15, bf16[12,12,512]{2,1,0:T(8,128)(2,1)} %bitcast.16, f32[144,1,32]{2,1,0:T(1,128)} %bitcast.18, ...), custom_call_target="tpu_custom_call" | custom-call | tf_op jit(solution)/shard_map/pallas_call | solution.py:664
  109.7 2.4 %shard_map.120 = (bf16[3,12,12,512]{3,2,1,0:T(8,128)(2,1)}, bf16[12,12,512]{2,1,0:T(8,128)(2,1)}, f32[2,512,128]{2,1,0:T(8,128)}, f32[2,512,128]{2,1,0:T(8,128)}, f32[144,1,32]{2,1,0:T(1,128)}) custom-call(bf16[3,12,12,512]{3,2,1,0:T(8,128)(2,1)} %get-tuple-element.15.refs_0_, bf16[12,12,512]{2,1,0:T(8,128)(2,1)} %get-tuple-element.16.refs_1_, ...), custom_call_target="tpu_custom_call" | custom-call | tf_op jit(solution)/shard_map/pallas_call | solution.py:733
